TPU v7x, 128 devices: a whole 4x4x4 slice. The times are simulated.
128 devices in a mesh: dp: 8 (over y, core), ctx: 16 (over z, x).
Axes of the slice: x: 4, y: 4, z: 4, core: 2. Of those that a mesh axis runs over, the one named last changes fastest.
Arguments:
- query: bfloat16 [8, 2048, 4096], P('dp', 'ctx'), may hold values from -140 to 140
- key_states: bfloat16 [8, 2048, 4096], P('dp', 'ctx'), may hold values from -7 to 7
- value_states: bfloat16 [8, 2048, 4096], P('dp', 'ctx'), may hold values from -6 to 6
- block_out: bfloat16 [8, 2048, 5120], P('dp', 'ctx'), may hold values from -6 to 6
- gate_mod: float32 [8, 5120], P('dp'), may hold values from 0.3 to 1.5
- head_mod: float32 [8, 2, 5120], P('dp'), may hold values from -4 to 4
- head_weight: bfloat16 [64, 5120], replicated, may hold values from -0.078125 to 0.078125
- proj_weight: bfloat16 [4096, 5120], P('ctx', 'dp'), may hold values from -0.09375 to 0.09375
- uncond_pred: float32 [8, 2048, 64], P('dp', 'ctx'), may hold values from -18 to 18
- target: float32 [8, 2048, 64], P('dp', 'ctx'), may hold values from -6 to 6
Outputs:
- grad_query: bfloat16 [8, 2048, 4096], P('dp', 'ctx')
- grad_key: bfloat16 [8, 2048, 4096], P('dp', 'ctx')
- grad_value: bfloat16 [8, 2048, 4096], P('dp', 'ctx')
- grad_stream: bfloat16 [8, 2048, 5120], P('dp', 'ctx')
- grad_proj: float32 [4096, 5120], P('ctx', 'dp')
- sample_loss: float32 [8], P('dp')
All inputs are finite; a program needn't handle non-finite values.
Results may differ from a plain program's by a relative error of at most 0.017.
Values may be sent and summed in bfloat16 or wider, within the bound.
A program may use at most 256 MiB of HBM per device.

v0:
```python
import jax
import jax.numpy as jnp
from jax import lax
from jax.sharding import PartitionSpec as P

HD = 128


guidance = 5.0
rescale_mix = 0.7
norm_epsilon = 1e-06
spread_epsilon = 1e-05


def sigma_of(first_sum, square_sum, cell_count):
    mean_value = first_sum / cell_count
    return jnp.sqrt(square_sum / cell_count - mean_value * mean_value + spread_epsilon)


def layer_stats(stream):
    values = stream.astype(jnp.float32)
    center = jnp.mean(values, axis=-1, keepdims=True)
    spread = jnp.mean(jnp.square(values - center), axis=-1, keepdims=True)
    inverse = lax.rsqrt(spread + norm_epsilon)
    return ((values - center) * inverse, inverse)


def stream_gradient(normed, inverse, cond_grad, head_weight, scale_row):
    head_grad = jnp.dot(cond_grad, head_weight, preferred_element_type=jnp.float32) * (
        1.0 + scale_row
    )
    mean_one = jnp.mean(head_grad, axis=-1, keepdims=True)
    mean_two = jnp.mean(head_grad * normed, axis=-1, keepdims=True)
    return (head_grad - mean_one - normed * mean_two) * inverse


def attend_backward(query_heads, key_heads, value_heads, out_grad):
    seq_rows, head_count, head_width = query_heads.shape
    factor = 1.0 / float(head_width) ** 0.5
    block_rows = min(512, seq_rows)
    block_count = seq_rows // block_rows
    features = head_count * head_width

    def step(running, index):
        grad_keys, grad_values = running
        start = index * block_rows
        query_block = lax.dynamic_slice_in_dim(query_heads, start, block_rows, 0)
        out_block = lax.dynamic_slice_in_dim(out_grad, start, block_rows, 0)
        scores = (
            jnp.einsum("qhd,khd->hqk", query_block, key_heads, preferred_element_type=jnp.float32)
            * factor
        )
        attn_probs = jax.nn.softmax(scores, axis=-1)
        probs_low = attn_probs.astype(jnp.bfloat16)
        attended = jnp.einsum(
            "hqk,khd->qhd", probs_low, value_heads, preferred_element_type=jnp.float32
        ).astype(jnp.bfloat16)
        grad_values = grad_values + jnp.einsum(
            "hqk,qhd->khd", probs_low, out_block, preferred_element_type=jnp.float32
        )
        prob_grad = jnp.einsum(
            "qhd,khd->hqk", out_block, value_heads, preferred_element_type=jnp.float32
        )
        row_delta = jnp.sum(attn_probs * prob_grad, axis=-1, keepdims=True)
        score_grad = (attn_probs * (prob_grad - row_delta) * factor).astype(jnp.bfloat16)
        query_grad = jnp.einsum(
            "hqk,khd->qhd", score_grad, key_heads, preferred_element_type=jnp.float32
        ).astype(jnp.bfloat16)
        grad_keys = grad_keys + jnp.einsum(
            "hqk,qhd->khd", score_grad, query_block, preferred_element_type=jnp.float32
        )
        return ((grad_keys, grad_values), (query_grad, attended))

    zero_heads = jnp.zeros((seq_rows, head_count, head_width), jnp.float32)
    finals, blocks = lax.scan(step, (zero_heads, zero_heads), jnp.arange(block_count))
    grad_keys, grad_values = finals
    grad_queries = blocks[0].reshape(seq_rows, features)
    attended_rows = blocks[1].reshape(seq_rows, features)
    return (
        grad_queries,
        grad_keys.reshape(seq_rows, features).astype(jnp.bfloat16),
        grad_values.reshape(seq_rows, features).astype(jnp.bfloat16),
        attended_rows,
    )


def per_device(
    query,
    key_states,
    value_states,
    block_out,
    gate_mod,
    head_mod,
    head_weight,
    proj_weight,
    uncond_pred,
    target,
):
    tok_rows = block_out.shape[1]
    groups = lax.axis_size("ctx")
    cell_count = tok_rows * groups * uncond_pred.shape[2]
    stream = block_out[0]
    proj_rows = lax.all_gather(proj_weight, "dp", axis=1, tiled=True)
    heads_in = (
        lax.all_to_all(query, "ctx", split_axis=2, concat_axis=1, tiled=True),
        lax.all_to_all(key_states, "ctx", split_axis=2, concat_axis=1, tiled=True),
        lax.all_to_all(value_states, "ctx", split_axis=2, concat_axis=1, tiled=True),
    )
    normed, inverse = layer_stats(stream)
    shift_row = head_mod[0, 0]
    scale_row = head_mod[0, 1]
    gate_row = gate_mod[0]
    hidden = (normed * (1.0 + scale_row) + shift_row).astype(jnp.bfloat16)
    cond_pred = jnp.einsum("td,pd->tp", hidden, head_weight, preferred_element_type=jnp.float32)
    uncond_rows = uncond_pred[0]
    target_rows = target[0]
    guided = uncond_rows + guidance * (cond_pred - uncond_rows)
    moment_sums = lax.psum(
        jnp.stack(
            [
                jnp.sum(cond_pred),
                jnp.sum(cond_pred * cond_pred),
                jnp.sum(guided),
                jnp.sum(guided * guided),
            ]
        ),
        "ctx",
    )
    sigma_cond = sigma_of(moment_sums[0], moment_sums[1], cell_count)
    sigma_guided = sigma_of(moment_sums[2], moment_sums[3], cell_count)
    mix_ratio = rescale_mix * sigma_cond / sigma_guided + (1.0 - rescale_mix)
    final = mix_ratio * guided
    final_grad = 2.0 * (final - target_rows)
    slope_pair = lax.psum(
        jnp.stack([jnp.sum(final_grad * guided), jnp.sum(jnp.square(final - target_rows))]), "ctx"
    )
    slope_sum = slope_pair[0]
    loss_value = slope_pair[1] / cell_count
    mean_guided = moment_sums[2] / cell_count
    mean_cond = moment_sums[0] / cell_count
    guided_coef = slope_sum * rescale_mix * sigma_cond / (cell_count * sigma_guided**3)
    guided_grad = mix_ratio * final_grad - guided_coef * (guided - mean_guided)
    cond_coef = slope_sum * rescale_mix / (cell_count * sigma_guided * sigma_cond)
    cond_grad = (guidance * guided_grad + cond_coef * (cond_pred - mean_cond)).astype(jnp.bfloat16)
    stream_grad_local = stream_gradient(normed, inverse, cond_grad, head_weight, scale_row)
    grad_stream = stream_grad_local.astype(jnp.bfloat16)
    proj_input = lax.all_gather(
        (gate_row * stream_grad_local).astype(jnp.bfloat16), "ctx", axis=0, tiled=True
    )
    attn_grad = jnp.einsum(
        "td,fd->tf", proj_input, proj_rows, preferred_element_type=jnp.float32
    ).astype(jnp.bfloat16)
    seq_rows = proj_input.shape[0]
    head_count = proj_rows.shape[0] // HD
    query_heads = heads_in[0][0].reshape(seq_rows, head_count, HD)
    key_heads = heads_in[1][0].reshape(seq_rows, head_count, HD)
    value_heads = heads_in[2][0].reshape(seq_rows, head_count, HD)
    out_grad = attn_grad.reshape(seq_rows, head_count, HD)
    grad_queries, grad_keys, grad_values, attended_rows = attend_backward(
        query_heads, key_heads, value_heads, out_grad
    )
    heads_out = (
        lax.all_to_all(grad_queries[None], "ctx", split_axis=1, concat_axis=2, tiled=True),
        lax.all_to_all(grad_keys[None], "ctx", split_axis=1, concat_axis=2, tiled=True),
        lax.all_to_all(grad_values[None], "ctx", split_axis=1, concat_axis=2, tiled=True),
    )
    grad_weight = jnp.einsum(
        "qf,qd->fd", attended_rows, proj_input, preferred_element_type=jnp.float32
    )
    grad_proj = lax.psum_scatter(
        grad_weight.astype(jnp.bfloat16), "dp", scatter_dimension=1, tiled=True
    ).astype(jnp.float32)
    sample_loss = jnp.reshape(loss_value, (1,))
    return (heads_out[0], heads_out[1], heads_out[2], grad_stream[None], grad_proj, sample_loss)


def solution(mesh):
    return jax.shard_map(
        per_device,
        mesh=mesh,
        in_specs=(
            P("dp", "ctx", None),
            P("dp", "ctx", None),
            P("dp", "ctx", None),
            P("dp", "ctx", None),
            P("dp", None),
            P("dp", None, None),
            P(),
            P("ctx", "dp"),
            P("dp", "ctx", None),
            P("dp", "ctx", None),
        ),
        out_specs=(
            P("dp", "ctx", None),
            P("dp", "ctx", None),
            P("dp", "ctx", None),
            P("dp", "ctx", None),
            P("ctx", "dp"),
            P("dp"),
        ),
        check_vma=False,
    )
```

profile of v0, /device:TPU:1, one launch (start us, length us, event | category | flops | bytes accessed | tf_op | source)
XLA Modules:
  0.0 621.8 jit_solution(13152901549069752722)
XLA Ops:
  15.5 35.3 %psum.14 = f32[4]{0:T(128)S(1)} all-reduce(f32[4]{0:T(128)S(1)} %pad_maximum_fusion), channel_id=1, replica_groups=mesh['dp'=8,'ctx'=16] {'ctx'}, use_global_device_ids=true, to_apply=%region_6.0 | all-reduce | flops 4 | bytes 32 | tf_op jit(solution)/shard_map/psum | solution.py:118
  57.4 28.5 %psum.15 = f32[2]{0:T(128)S(1)} all-reduce(f32[2]{0:T(128)S(1)} %pad_maximum_fusion.1), channel_id=1, replica_groups=mesh['dp'=8,'ctx'=16] {'ctx'}, use_global_device_ids=true, to_apply=%region_9.0 | all-reduce | flops 2 | bytes 16 | tf_op jit(solution)/shard_map/psum | solution.py:134
  98.3 23.4 %reduce.1 = bf16[4096,128]{1,0:T(8,128)(2,1)} reduce(bf16[4096,1,128]{2,1,0:T(2,128)(2,1)S(1)} %bitcast.172, bf16[]{:T(256)} %broadcast.105), dimensions={1}, to_apply=%bitcast.119.reduce_sub_computation | reduce | bytes 2097154
  133.4 23.4 %reduce.2 = bf16[4096,128]{1,0:T(8,128)(2,1)} reduce(bf16[4096,1,128]{2,1,0:T(2,128)(2,1)S(1)} %bitcast.176, bf16[]{:T(256)} %broadcast.105), dimensions={1}, to_apply=%bitcast.121.reduce_sub_computation | reduce | bytes 2097154
  171.0 23.4 %reduce.3 = bf16[4096,128]{1,0:T(8,128)(2,1)} reduce(bf16[4096,1,128]{2,1,0:T(2,128)(2,1)S(1)} %bitcast.177, bf16[]{:T(256)} %broadcast.105), dimensions={1}, to_apply=%bitcast.123.reduce_sub_computation | reduce | bytes 2097154
  217.1 9.7 %all-to-all-done.2 = bf16[16,2,16384]{2,1,0:T(2,128)(2,1)} async-done(((bf16[16,2,16384]{2,1,0:T(2,128)(2,1)}), bf16[16,2,16384]{2,1,0:T(2,128)(2,1)}, u32[]{:S(2)}, u32[]{:S(2)}) %all-to-all-start.2) | async-done | bytes 1048608 | tf_op jit(solution)/shard_map/all_to_all | solution.py:107
  233.1 32.8 %all-gather.3.cloned.1.call-done = bf16[2048,5120]{1,0:T(8,128)(2,1)} async-done(((bf16[128,5120]{1,0:T(8,128)(2,1)}), bf16[2048,5120]{1,0:T(8,128)(2,1)}) %all-gather.3.cloned.1.call-update) | async-done | bytes 20971536 | tf_op jit(solution)/shard_map/all_gather | solution.py:147
  266.0 10.6 %convolution_convert_fusion.1 = bf16[2048,256]{0,1:T(8,128)(2,1)S(1)} fusion(bf16[2048,5120]{1,0:T(8,128)(2,1)} %all-gather.3.cloned.1.call-done, bf16[256,5120]{1,0:T(8,128)(2,1)} %all-gather.5.cloned.1.call-done), kind=kOutput, calls=%fused_computation.60 | convolution fusion | flops 5369233408 | bytes 24641536 | tf_op jit(solution)/shard_map/td,fd->tf/dot_general | solution.py:150
  276.6 218.1 %while.17 = (s32[]{:T(128)}, f32[2048,2,128]{0,2,1:T(8,128)}, f32[2048,2,128]{0,2,1:T(8,128)}, bf16[4,512,2,128]{3,2,1,0:T(2,128)(2,1)}, bf16[4,512,2,128]{3,2,1...) while((s32[]{:T(128)}, f32[2048,2,128]{0,2,1:T(8,128)}, ...), condition=%wide.region_16.17_spmd.clone, body=%wide.region_12.16_spmd.clone.sunk | while | flops 3267633152 | bytes 132669704 | solution.py:75
  282.6 7.3 %fusion.140 = (f32[2,512]{1,0:T(2,128)S(1)}, f32[2,512,2048]{2,1,0:T(8,128)}) fusion(bf16[2048,2,128]{2,0,1:T(8,128)(2,1)} %get-tuple-element.320, bf16[2048,2,128]{0,2,1:T(8,128)(2,1)} %get-tuple-element.319, s32[]{:T(128)S(6)} %select_n.6), kind=kOutput, calls=%fused_computation.92.clone.1 | convolution fusion | flops 543164416 | bytes 9703428 | tf_op jit(solution)/shard_map/while/body/eval_jaxpr/sub | solution.py:53
  289.9 18.1 %fusion.141 = f32[2048,2,128]{0,2,1:T(8,128)} fusion(f32[2,512,2048]{2,1,0:T(8,128)} %fusion.139, f32[2048,2,128]{0,2,1:T(8,128)} %get-tuple-element.300, pred[]{:T(512)S(6)} %compare.3, bf16[2048,2,128]{0,2,1:T(8,128)(2,1)} %get-tuple-element.319, s32[]{:T(128)S(6)} %select_n.6, f32[2,512,2048]{2,1,0:T(8,128)} %get-tuple-element.281, ...), kind=kOutput, calls=%fused_computation.15.clone.1 | convolution fusion | flops 552602624 | bytes 38019076 | tf_op jit(solution)/shard_map/while/body/eval_jaxpr/hqk,qhd->khd/dot_general | solution.py:69
  315.9 13.2 %fusion.144 = bf16[1,512,2,128]{3,1,2,0:T(8,128)(2,1)S(1)} fusion(bf16[2048,2,128]{2,0,1:T(8,128)(2,1)} %get-tuple-element.320, f32[2,512,2048]{2,1,0:T(8,128)} %fusion.139, f32[2,512,2048]{2,1,0:T(8,128)} %get-tuple-element.281, f32[2,512]{1,0:T(2,128)S(1)} %get-tuple-element.282), kind=kOutput, calls=%fused_computation.21.clone.1 | convolution fusion | flops 551685120 | bytes 18092032 | tf_op jit(solution)/shard_map/while/body/eval_jaxpr/hqk,khd->qhd/dot_general | solution.py:66
  336.2 7.3 %fusion.140 = (f32[2,512]{1,0:T(2,128)S(1)}, f32[2,512,2048]{2,1,0:T(8,128)}) fusion(bf16[2048,2,128]{2,0,1:T(8,128)(2,1)} %get-tuple-element.320, bf16[2048,2,128]{0,2,1:T(8,128)(2,1)} %get-tuple-element.319, s32[]{:T(128)S(6)} %select_n.6), kind=kOutput, calls=%fused_computation.92.clone.1 | convolution fusion | flops 543164416 | bytes 9703428 | tf_op jit(solution)/shard_map/while/body/eval_jaxpr/sub | solution.py:53
  343.6 18.6 %fusion.141 = f32[2048,2,128]{0,2,1:T(8,128)} fusion(f32[2,512,2048]{2,1,0:T(8,128)} %fusion.139, f32[2048,2,128]{0,2,1:T(8,128)} %get-tuple-element.300, pred[]{:T(512)S(6)} %compare.3, bf16[2048,2,128]{0,2,1:T(8,128)(2,1)} %get-tuple-element.319, s32[]{:T(128)S(6)} %select_n.6, f32[2,512,2048]{2,1,0:T(8,128)} %get-tuple-element.281, ...), kind=kOutput, calls=%fused_computation.15.clone.1 | convolution fusion | flops 552602624 | bytes 38019076 | tf_op jit(solution)/shard_map/while/body/eval_jaxpr/hqk,qhd->khd/dot_general | solution.py:69
  370.6 13.2 %fusion.144 = bf16[1,512,2,128]{3,1,2,0:T(8,128)(2,1)S(1)} fusion(bf16[2048,2,128]{2,0,1:T(8,128)(2,1)} %get-tuple-element.320, f32[2,512,2048]{2,1,0:T(8,128)} %fusion.139, f32[2,512,2048]{2,1,0:T(8,128)} %get-tuple-element.281, f32[2,512]{1,0:T(2,128)S(1)} %get-tuple-element.282), kind=kOutput, calls=%fused_computation.21.clone.1 | convolution fusion | flops 551685120 | bytes 18092032 | tf_op jit(solution)/shard_map/while/body/eval_jaxpr/hqk,khd->qhd/dot_general | solution.py:66
  398.3 18.6 %fusion.141 = f32[2048,2,128]{0,2,1:T(8,128)} fusion(f32[2,512,2048]{2,1,0:T(8,128)} %fusion.139, f32[2048,2,128]{0,2,1:T(8,128)} %get-tuple-element.300, pred[]{:T(512)S(6)} %compare.3, bf16[2048,2,128]{0,2,1:T(8,128)(2,1)} %get-tuple-element.319, s32[]{:T(128)S(6)} %select_n.6, f32[2,512,2048]{2,1,0:T(8,128)} %get-tuple-element.281, ...), kind=kOutput, calls=%fused_computation.15.clone.1 | convolution fusion | flops 552602624 | bytes 38019076 | tf_op jit(solution)/shard_map/while/body/eval_jaxpr/hqk,qhd->khd/dot_general | solution.py:69
  425.4 13.2 %fusion.144 = bf16[1,512,2,128]{3,1,2,0:T(8,128)(2,1)S(1)} fusion(bf16[2048,2,128]{2,0,1:T(8,128)(2,1)} %get-tuple-element.320, f32[2,512,2048]{2,1,0:T(8,128)} %fusion.139, f32[2,512,2048]{2,1,0:T(8,128)} %get-tuple-element.281, f32[2,512]{1,0:T(2,128)S(1)} %get-tuple-element.282), kind=kOutput, calls=%fused_computation.21.clone.1 | convolution fusion | flops 551685120 | bytes 18092032 | tf_op jit(solution)/shard_map/while/body/eval_jaxpr/hqk,khd->qhd/dot_general | solution.py:66
  445.7 7.3 %fusion.140 = (f32[2,512]{1,0:T(2,128)S(1)}, f32[2,512,2048]{2,1,0:T(8,128)}) fusion(bf16[2048,2,128]{2,0,1:T(8,128)(2,1)} %get-tuple-element.320, bf16[2048,2,128]{0,2,1:T(8,128)(2,1)} %get-tuple-element.319, s32[]{:T(128)S(6)} %select_n.6), kind=kOutput, calls=%fused_computation.92.clone.1 | convolution fusion | flops 543164416 | bytes 9703428 | tf_op jit(solution)/shard_map/while/body/eval_jaxpr/sub | solution.py:53
  453.1 18.7 %fusion.141 = f32[2048,2,128]{0,2,1:T(8,128)} fusion(f32[2,512,2048]{2,1,0:T(8,128)} %fusion.139, f32[2048,2,128]{0,2,1:T(8,128)} %get-tuple-element.300, pred[]{:T(512)S(6)} %compare.3, bf16[2048,2,128]{0,2,1:T(8,128)(2,1)} %get-tuple-element.319, s32[]{:T(128)S(6)} %select_n.6, f32[2,512,2048]{2,1,0:T(8,128)} %get-tuple-element.281, ...), kind=kOutput, calls=%fused_computation.15.clone.1 | convolution fusion | flops 552602624 | bytes 38019076 | tf_op jit(solution)/shard_map/while/body/eval_jaxpr/hqk,qhd->khd/dot_general | solution.py:69
  480.2 13.2 %fusion.144 = bf16[1,512,2,128]{3,1,2,0:T(8,128)(2,1)S(1)} fusion(bf16[2048,2,128]{2,0,1:T(8,128)(2,1)} %get-tuple-element.320, f32[2,512,2048]{2,1,0:T(8,128)} %fusion.139, f32[2,512,2048]{2,1,0:T(8,128)} %get-tuple-element.281, f32[2,512]{1,0:T(2,128)S(1)} %get-tuple-element.282), kind=kOutput, calls=%fused_computation.21.clone.1 | convolution fusion | flops 551685120 | bytes 18092032 | tf_op jit(solution)/shard_map/while/body/eval_jaxpr/hqk,khd->qhd/dot_general | solution.py:66
  494.7 10.4 %convolution_convert_fusion = bf16[256,5120]{1,0:T(8,128)(2,1)S(1)} fusion(bf16[2048,5120]{1,0:T(8,128)(2,1)} %all-gather.3.cloned.1.call-done, bf16[256,8,2,128]{3,2,1,0:T(2,128)(2,1)} %bitcast.190), kind=kOutput, calls=%fused_computation.43 | convolution fusion | flops 5370019840 | bytes 24641536 | tf_op jit(solution)/shard_map/qf,qd->fd/dot_general | solution.py:167
  514.1 11.6 %reduce.4 = bf16[2048,256]{1,0:T(8,128)(2,1)} reduce(bf16[2048,1,256]{2,1,0:T(2,128)(2,1)S(1)} %bitcast.174, bf16[]{:T(256)} %broadcast.105), dimensions={1}, to_apply=%bitcast.125.reduce_sub_computation | reduce | bytes 2097154
  538.8 11.6 %reduce.5 = bf16[2048,256]{1,0:T(8,128)(2,1)} reduce(bf16[2048,1,256]{2,1,0:T(2,128)(2,1)S(1)} %bitcast.175, bf16[]{:T(256)} %broadcast.105), dimensions={1}, to_apply=%bitcast.127.reduce_sub_computation | reduce | bytes 2097154
  565.3 11.6 %reduce.6 = bf16[2048,256]{1,0:T(8,128)(2,1)} reduce(bf16[2048,1,256]{2,1,0:T(2,128)(2,1)S(1)} %bitcast.173, bf16[]{:T(256)} %broadcast.105), dimensions={1}, to_apply=%bitcast.129.reduce_sub_computation | reduce | bytes 2097154
  (130 shorter events, 216.0 us)
Async XLA Ops:
  7.2 4.3 copy-start
  7.2 4.3 copy-start.2
  7.2 4.2 copy-start.6
  7.2 4.3 copy-start.8
  7.2 225.9 %all-gather.5.cloned.1.call-start = ((), (), s32[]{:S(2)}) async-start(), calls=%async_computation.8 | async-start | bytes 2949120 | tf_op jit(solution)/shard_map/all_gather | solution.py:103
  7.9 258.0 %all-gather.3.cloned.1.call-start = ((), (), s32[]{:S(2)}) async-start(), calls=%async_computation.7 | async-start | bytes 22282240 | tf_op jit(solution)/shard_map/all_gather | solution.py:147
  9.6 45.8 %copy-start.5 = (f32[1,128,64]{1,2,0:T(8,128)S(1)}, f32[1,128,64]{1,2,0:T(8,128)}, u32[]{:S(2)}) copy-start(f32[1,128,64]{1,2,0:T(8,128)} %param.21) | copy-start | bytes 98308
  89.5 2.0 copy-start.7
  123.8 35.4 %all-to-all-start = ((bf16[16,2,16384]{2,1,0:T(2,128)(2,1)}), bf16[16,2,16384]{2,1,0:T(2,128)(2,1)}, u32[]{:S(2)}, u32[]{:S(2)}) async-start(bf16[16,2,16384]{2,1,0:T(2,128)(2,1)} %reshape.111), calls=%async_computation | async-start | bytes 2097152 | tf_op jit(solution)/shard_map/all_to_all | solution.py:105
  159.2 37.3 %all-to-all-start.1 = ((bf16[16,2,16384]{2,1,0:T(2,128)(2,1)}), bf16[16,2,16384]{2,1,0:T(2,128)(2,1)}, u32[]{:S(2)}, u32[]{:S(2)}) async-start(bf16[16,2,16384]{2,1,0:T(2,128)(2,1)} %reshape.113), calls=%async_computation.1 | async-start | bytes 2097152 | tf_op jit(solution)/shard_map/all_to_all | solution.py:106
  196.5 30.2 %all-to-all-start.2 = ((bf16[16,2,16384]{2,1,0:T(2,128)(2,1)}), bf16[16,2,16384]{2,1,0:T(2,128)(2,1)}, u32[]{:S(2)}, u32[]{:S(2)}) async-start(bf16[16,2,16384]{2,1,0:T(2,128)(2,1)} %reshape.115), calls=%async_computation.2 | async-start | bytes 2097152 | tf_op jit(solution)/shard_map/all_to_all | solution.py:107
  203.2 408.5 %reduce-scatter.4.cloned.1.call-start = ((), (), s32[]{:S(2)}) async-start(), calls=%async_computation.9 | async-start | bytes 2949120
  308.0 6.5 %copy-start.9 = (f32[2,512,2048]{2,1,0:T(8,128)S(1)}, f32[2,512,2048]{2,1,0:T(8,128)}, u32[]{:S(2)}) copy-start(f32[2,512,2048]{2,1,0:T(8,128)} %get-tuple-element.281) | copy-start | bytes 25165828 | tf_op jit(solution)/shard_map/while
  362.2 7.1 %copy-start.9 = (f32[2,512,2048]{2,1,0:T(8,128)S(1)}, f32[2,512,2048]{2,1,0:T(8,128)}, u32[]{:S(2)}) copy-start(f32[2,512,2048]{2,1,0:T(8,128)} %get-tuple-element.281) | copy-start | bytes 25165828 | tf_op jit(solution)/shard_map/while
  416.9 7.1 %copy-start.9 = (f32[2,512,2048]{2,1,0:T(8,128)S(1)}, f32[2,512,2048]{2,1,0:T(8,128)}, u32[]{:S(2)}) copy-start(f32[2,512,2048]{2,1,0:T(8,128)} %get-tuple-element.281) | copy-start | bytes 25165828 | tf_op jit(solution)/shard_map/while
  471.7 7.1 %copy-start.9 = (f32[2,512,2048]{2,1,0:T(8,128)S(1)}, f32[2,512,2048]{2,1,0:T(8,128)}, u32[]{:S(2)}) copy-start(f32[2,512,2048]{2,1,0:T(8,128)} %get-tuple-element.281) | copy-start | bytes 25165828 | tf_op jit(solution)/shard_map/while
  525.7 7.4 %copy-start.3 = (f32[2048,2,128]{0,2,1:T(8,128)S(1)}, f32[2048,2,128]{0,2,1:T(8,128)}, u32[]{:S(2)}) copy-start(f32[2048,2,128]{0,2,1:T(8,128)} %get-tuple-element.62) | copy-start | bytes 6291460
  528.0 24.7 %all-to-all-start.3 = ((bf16[16,2,16384]{2,1,0:T(2,128)(2,1)}), bf16[16,2,16384]{2,1,0:T(2,128)(2,1)}, u32[]{:S(2)}, u32[]{:S(2)}) async-start(bf16[16,2,16384]{2,1,0:T(2,128)(2,1)} %reshape.117), calls=%async_computation.3 | async-start | bytes 2097152 | tf_op jit(solution)/shard_map/all_to_all | solution.py:163
  550.4 9.2 %copy-start.4 = (f32[2048,2,128]{0,2,1:T(8,128)S(1)}, f32[2048,2,128]{0,2,1:T(8,128)}, u32[]{:S(2)}) copy-start(f32[2048,2,128]{0,2,1:T(8,128)} %get-tuple-element.63) | copy-start | bytes 6291460
  552.6 26.4 %all-to-all-start.4 = ((bf16[16,2,16384]{2,1,0:T(2,128)(2,1)}), bf16[16,2,16384]{2,1,0:T(2,128)(2,1)}, u32[]{:S(2)}, u32[]{:S(2)}) async-start(bf16[16,2,16384]{2,1,0:T(2,128)(2,1)} %reshape.119), calls=%async_computation.4 | async-start | bytes 2097152 | tf_op jit(solution)/shard_map/all_to_all | solution.py:164
  579.0 24.2 %all-to-all-start.5 = ((bf16[16,2,16384]{2,1,0:T(2,128)(2,1)}), bf16[16,2,16384]{2,1,0:T(2,128)(2,1)}, u32[]{:S(2)}, u32[]{:S(2)}) async-start(bf16[16,2,16384]{2,1,0:T(2,128)(2,1)} %reshape.121), calls=%async_computation.5 | async-start | bytes 2097152 | tf_op jit(solution)/shard_map/all_to_all | solution.py:165
  608.7 5.1 copy-start.1
Sparse Core Ops, SparseCore 0:
  9.7 30.0 all-gather.4
  92.9 173.0 all-gather.2
  507.9 31.4 reduce-scatter.3
where the time goes:
time: 632 us; the launch traced here: 622 us
  matrix products  228 us (36%)
  other arithmetic  119 us (19%)
  local copies, waits for them, and re-layouts  105 us (17%)
  blocking collectives  63.7 us (10%)
  waiting for transfers between devices  43.2 us (7%)
  starting transfers between devices  37.2 us (6%)
  between operations  22.4 us (4%)
    unnamed x8, other arithmetic  105 us
    dot_general x4, matrix products, step(): jnp.einsum('hqk,qhd->khd', score_grad, query_block, preferred_element_typ...  74 us
    unnamed x47, local copies, waits for them, and re-layouts  68.5 us
    dot_general x4, matrix products, step(): jnp.einsum('hqk,khd->qhd', score_grad, key_heads, preferred_element_type=...  52.7 us
    psum x1, blocking collectives, per_device(): lax.psum(jnp.stack([jnp.sum(cond_pred), jnp.sum(cond_pred * cond_pred), j...  35.3 us
    all_gather x1, waiting for transfers between devices, per_device(): lax.all_gather((gate_row * stream_grad_local).astype(jnp.bfloat16), 'ctx'...  32.8 us
    sub x4, matrix products, step(): attn_probs = jax.nn.softmax(scores, axis=-1)  29.3 us
    psum x1, blocking collectives, per_device(): lax.psum(jnp.stack([jnp.sum(final_grad * guided), jnp.sum(jnp.square(fina...  28.5 us
  transfers between devices with their start and end apart: 9, of which 2 were waited for; matrix products, arithmetic and copies ran while one was open for 34% of the time, Pallas kernels for 0%

commit v1 on v0

v1 whole, which is shorter than its diff:
```python
import functools

import jax
import jax.numpy as jnp
from jax import lax
from jax.experimental import pallas as pl
from jax.experimental.pallas import tpu as pltpu
from jax.sharding import PartitionSpec as P

HD = 128
PAIR = 2 * HD
SHARDS = 16
SCALE = 1.0 / float(HD) ** 0.5
EXP2_SCALE = 1.4426950408889634 * SCALE
MESH = pl.DeviceIdType.MESH

guidance = 5.0
rescale_mix = 0.7
norm_epsilon = 1e-06
spread_epsilon = 1e-05


def dot_nt(left, right):
    return lax.dot_general(left, right, (((1,), (1,)), ((), ())), preferred_element_type=jnp.float32)


def dot_nn(left, right):
    return lax.dot_general(left, right, (((1,), (0,)), ((), ())), preferred_element_type=jnp.float32)


def sigma_of(first_sum, square_sum, cell_count):
    mean_value = first_sum / cell_count
    return jnp.sqrt(square_sum / cell_count - mean_value * mean_value + spread_epsilon)


class Place:
    def __init__(self):
        dp = lax.axis_index("dp")
        ctx = lax.axis_index("ctx")
        self.dp, self.ctx = dp, ctx
        self.y, self.core = dp // 2, dp % 2
        self.z, self.x = ctx // 4, ctx % 4
        self.half = self.x // 2
        self.away = (self.core + self.half) % 2
        self.slot = self.z * 4 + self.x + self.away * (3 - 2 * self.x)
        self.mirror = self.z * 4 + 3 - self.x


def slot_of(z, x, core):
    away = (core + x // 2) % 2
    return z * 4 + x + away * (3 - 2 * x)


def greet(place):
    barrier = pltpu.get_barrier_semaphore()

    @pl.loop(0, 2 * SHARDS)
    def _(index):
        core, ctx = index // SHARDS, index % SHARDS
        own = jnp.logical_and(core == place.core, ctx == place.ctx)

        @pl.when(jnp.logical_not(own))
        def _():
            pl.semaphore_signal(
                barrier, inc=1, device_id=(place.y * 2 + core, ctx), device_id_type=MESH
            )

    for step in range(1, 4):
        other = ((place.y + step) % 4) * 2 + place.core
        pl.semaphore_signal(barrier, inc=1, device_id=(other, place.ctx), device_id_type=MESH)
    pl.semaphore_wait(barrier, 2 * SHARDS - 1 + 3)


def remote(src, dst, send_sem, recv_sem, dp, ctx):
    return pltpu.make_async_remote_copy(
        src_ref=src, dst_ref=dst, send_sem=send_sem, recv_sem=recv_sem, device_id=(dp, ctx), device_id_type=MESH
    )


def wait_bytes(ref, sem):
    pltpu.make_async_copy(ref, ref, sem).wait()


def rows_of(index, count):
    return pl.ds(pl.multiple_of(index * count, count), count)


def head_kernel(
    q_ref, k_ref, v_ref, stream_ref, gate_ref, mod_ref, hw_ref, pw_ref, uncond_ref, target_ref,
    qh_ref, kh_ref, vh_ref, w_ref, p_ref, gs_ref, loss_ref,
    moments, losses, mine, mine_loss, p_buf,
    a2a_send, a2a_recv, w_send, w_recv, m_send, m_recv, l_send, l_recv, p_send, p_recv,
):
    place = Place()
    tokens = stream_ref.shape[1]
    chunk = pw_ref.shape[1]
    cell_count = float(tokens * SHARDS * uncond_ref.shape[2])
    greet(place)

    def send_heads(src, dst, index):
        @pl.loop(0, SHARDS)
        def _(step):
            z = (place.z + step // 4) % 4
            x = 2 * place.core + (step // 2 + place.x) % 2
            core = (step + place.core) % 2
            slot = slot_of(z, x, core)
            own = jnp.logical_and(core == place.core, z * 4 + x == place.ctx)
            part = src.at[0, :, rows_of(slot, PAIR)]
            land = dst.at[rows_of(place.ctx, tokens), :]

            @pl.when(own)
            def _():
                pltpu.make_async_copy(part, land, a2a_recv.at[index]).start()

            @pl.when(jnp.logical_not(own))
            def _():
                remote(part, land, a2a_send.at[index], a2a_recv.at[index], place.y * 2 + core, z * 4 + x).start()

    own_cols = w_ref.at[:, rows_of(place.dp, chunk)]
    user = place.y * 2 + place.half

    @pl.when(place.away == 0)
    def _():
        pltpu.make_async_copy(pw_ref, own_cols, w_recv.at[0]).start()

    @pl.when(place.away == 1)
    def _():
        remote(pw_ref, own_cols, w_send.at[0], w_recv.at[0], user, place.ctx).start()

    remote(pw_ref, own_cols, w_send.at[1], w_recv.at[0], user, place.mirror).start()
    send_heads(q_ref, qh_ref, 0)
    send_heads(k_ref, kh_ref, 1)

    values = stream_ref[0].astype(jnp.float32)
    center = jnp.mean(values, axis=-1, keepdims=True)
    spread = jnp.mean(jnp.square(values - center), axis=-1, keepdims=True)
    inverse = lax.rsqrt(spread + norm_epsilon)
    normed = (values - center) * inverse
    scale_row = 1.0 + mod_ref[0, 1:2, :]
    hidden = (normed * scale_row + mod_ref[0, 0:1, :]).astype(jnp.bfloat16)
    cond_pred = dot_nt(hidden, hw_ref[...])
    uncond = uncond_ref[0]
    target = target_ref[0]
    guided = uncond + guidance * (cond_pred - uncond)

    def total(array):
        return jnp.sum(jnp.sum(array, axis=0, keepdims=True), axis=1, keepdims=True)

    lane = lax.broadcasted_iota(jnp.int32, (8, 128), 1)
    tile = jnp.zeros((8, 128), jnp.float32)
    for index, array in enumerate(
        (cond_pred, cond_pred * cond_pred, guided, guided * guided, guided * target)
    ):
        tile = jnp.where(lane == index, total(array), tile)
    mine[...] = tile

    def share(src, dst, send, recv):
        @pl.loop(1, SHARDS)
        def _(step):
            ctx = (place.ctx + step) % SHARDS
            remote(src, dst.at[place.ctx], send, recv, place.dp, ctx).start()

    def settle(dst, send, recv):
        wait_bytes(dst.at[pl.ds(0, SHARDS - 1)], recv)
        wait_bytes(dst.at[pl.ds(0, SHARDS - 1)], send)

    moments[place.ctx] = tile
    share(mine, moments, m_send, m_recv)
    send_heads(v_ref, vh_ref, 2)

    pair = w_ref.at[:, rows_of(place.y, 2 * chunk)]
    wait_bytes(pair, w_recv.at[0])
    for step in range(1, 4):
        other = ((place.y + step) % 4) * 2 + place.core
        remote(pair, pair, w_send.at[2], w_recv.at[1], other, place.ctx).start()

    settle(moments, m_send, m_recv)
    sums = jnp.sum(moments[...], axis=0)
    sum_cond, square_cond, sum_guided, square_guided, cross = [sums[0:1, i : i + 1] for i in range(5)]
    sigma_cond = sigma_of(sum_cond, square_cond, cell_count)
    sigma_guided = sigma_of(sum_guided, square_guided, cell_count)
    mix_ratio = rescale_mix * sigma_cond / sigma_guided + (1.0 - rescale_mix)
    final = mix_ratio * guided
    final_grad = 2.0 * (final - target)
    loss_tile = jnp.broadcast_to(total(jnp.square(final - target)), (8, 128))
    mine_loss[...] = loss_tile
    losses[place.ctx] = loss_tile
    share(mine_loss, losses, l_send, l_recv)
    slope_sum = 2.0 * (mix_ratio * square_guided - cross)
    guided_coef = slope_sum * rescale_mix * sigma_cond / (cell_count * sigma_guided * sigma_guided * sigma_guided)
    guided_grad = mix_ratio * final_grad - guided_coef * (guided - sum_guided / cell_count)
    cond_coef = slope_sum * rescale_mix / (cell_count * sigma_guided * sigma_cond)
    cond_grad = (guidance * guided_grad + cond_coef * (cond_pred - sum_cond / cell_count)).astype(jnp.bfloat16)
    head_grad = dot_nn(cond_grad, hw_ref[...]) * scale_row
    mean_one = jnp.mean(head_grad, axis=-1, keepdims=True)
    mean_two = jnp.mean(head_grad * normed, axis=-1, keepdims=True)
    stream_grad = (head_grad - mean_one - normed * mean_two) * inverse
    p_buf[...] = (gate_ref[...] * stream_grad).astype(jnp.bfloat16)

    @pl.when(place.away == 0)
    def _():
        pltpu.make_async_copy(p_buf, p_ref, p_recv).start()

    @pl.when(place.away == 1)
    def _():
        remote(p_buf, p_ref, p_send, p_recv, place.dp + 1 - 2 * place.core, place.mirror).start()

    gs_ref[0] = stream_grad.astype(jnp.bfloat16)
    settle(losses, l_send, l_recv)
    loss_ref[...] = jnp.sum(losses[...], axis=0) / cell_count

    wait_bytes(p_ref, p_recv)
    wait_bytes(w_ref.at[:, pl.ds(0, 6 * chunk)], w_recv.at[1])
    for index, ref in enumerate((qh_ref, kh_ref, vh_ref)):
        wait_bytes(ref, a2a_recv.at[index])

        @pl.loop(0, SHARDS - 1 + place.away)
        def _(step):
            wait_bytes(ref.at[pl.ds(0, tokens), :], a2a_send.at[index])

    wait_bytes(w_ref.at[:, pl.ds(0, chunk)], w_send.at[1])
    wait_bytes(w_ref.at[:, pl.ds(0, 6 * chunk)], w_send.at[2])

    @pl.when(place.away == 1)
    def _():
        wait_bytes(w_ref.at[:, pl.ds(0, chunk)], w_send.at[0])
        wait_bytes(p_ref, p_send)


def run_head(query, key, value, stream, gate, mod, head_weight, proj_weight, uncond, target):
    tokens, features = query.shape[1:]
    width = stream.shape[2]
    vmem = pl.BlockSpec(memory_space=pltpu.VMEM)
    hbm = pl.BlockSpec(memory_space=pl.ANY)
    slab = jax.ShapeDtypeStruct((tokens * SHARDS, PAIR), jnp.bfloat16)
    dma = pltpu.SemaphoreType.DMA
    return pl.pallas_call(
        head_kernel,
        out_shape=[
            slab, slab, slab,
            jax.ShapeDtypeStruct((PAIR, width), jnp.bfloat16),
            jax.ShapeDtypeStruct((tokens, width), jnp.bfloat16),
            jax.ShapeDtypeStruct(stream.shape, jnp.bfloat16),
            jax.ShapeDtypeStruct((8, 128), jnp.float32),
        ],
        in_specs=[hbm] * 3 + [vmem] * 7,
        out_specs=[hbm] * 5 + [vmem] * 2,
        scratch_shapes=[
            pltpu.VMEM((SHARDS, 8, 128), jnp.float32),
            pltpu.VMEM((SHARDS, 8, 128), jnp.float32),
            pltpu.VMEM((8, 128), jnp.float32),
            pltpu.VMEM((8, 128), jnp.float32),
            pltpu.VMEM((tokens, width), jnp.bfloat16),
            dma((3,)), dma((3,)), dma((3,)), dma((2,)),
            dma, dma, dma, dma, dma, dma,
        ],
        compiler_params=pltpu.CompilerParams(
            collective_id=0, has_side_effects=True, vmem_limit_bytes=60 * 2**20
        ),
    )(query, key, value, stream, gate, mod, head_weight, proj_weight, uncond, target)


def attention_kernel(
    q_ref, k_ref, v_ref, w_ref, own_ref,
    gq_ref, gk_ref, gv_ref, gp_ref,
    p_ref, v_ones, dk_sum, dv_sum, turned, dq_out, dk_out, dv_out, g_out, g_in, g_pair, g_last,
    ag_send, side_recv, next_recv, next2_recv, far_recv, sib_recv, own_sem,
    out_send, out_recv, g_send, g_recv, h_send, h_recv,
):
    place = Place()
    seq = q_ref.shape[0]
    tokens = seq // SHARDS
    width = p_ref.shape[1]
    half = tokens // 2
    tile = 2 * tokens
    greet(place)

    side_x = place.x + 1 - 2 * (place.x % 2)
    side = place.z * 4 + side_x
    sibling = place.dp + 1 - 2 * place.core

    def beside(step):
        return ((place.z + step) % 4) * 4 + place.x

    def block(z_step, x):
        return rows_of(slot_of((place.z + z_step) % 4, x, place.core), tokens)

    def spread(src, rows, recv, index):
        dst = p_ref.at[rows, :]
        remote(src, dst, ag_send.at[0], recv.at[3], place.dp, beside(1)).start()
        remote(src, dst, ag_send.at[0], recv.at[1], place.dp, beside(3)).start()

    def to_sibling(rows, index):
        remote(p_ref.at[rows, :], p_ref.at[rows, :], ag_send.at[1], sib_recv.at[index], sibling, place.ctx).start()

    def relay(x, far):
        low = p_ref.at[pl.ds(pl.multiple_of(slot_of((place.z + 3) % 4, x, place.core) * tokens, tokens), half), :]
        high = p_ref.at[
            pl.ds(pl.multiple_of(slot_of((place.z + 1) % 4, x, place.core) * tokens + half, half), half), :
        ]
        remote(low, low, ag_send.at[2], far_recv.at[far], place.dp, beside(1)).start()
        remote(high, high, ag_send.at[2], far_recv.at[far], place.dp, beside(3)).start()

    own_rows = block(0, place.x)
    side_rows = block(0, side_x)
    dst = p_ref.at[own_rows, :]
    remote(own_ref, dst, ag_send.at[1], side_recv, place.dp, side).start()
    spread(own_ref, own_rows, next_recv, 0)
    remote(own_ref, dst, ag_send.at[1], sib_recv.at[0], sibling, place.ctx).start()
    keep = pltpu.make_async_copy(own_ref, dst, own_sem)
    keep.start()

    for head in range(2):
        cols = slice(head * HD, (head + 1) * HD)
        v_ones[head, :, 0:HD] = v_ref[:, cols]
        v_ones[head, :, HD : 2 * HD] = jnp.ones((seq, HD), jnp.bfloat16)
    dk_sum[...] = jnp.zeros_like(dk_sum)
    dv_sum[...] = jnp.zeros_like(dv_sum)
    keep.wait()

    wait_bytes(dst, side_recv)
    spread(p_ref.at[side_rows, :], side_rows, next2_recv, 0)
    to_sibling(side_rows, 0)

    def send_rows(src, dst_ref, shard, index):
        own = jnp.logical_and(place.away == 0, shard == place.ctx)
        part = src.at[rows_of(shard, tokens), :]
        land = dst_ref.at[0, :, rows_of(place.slot, PAIR)]

        @pl.when(own)
        def _():
            pltpu.make_async_copy(part, land, out_recv.at[index]).start()

        @pl.when(jnp.logical_not(own))
        def _():
            remote(part, land, out_send.at[index], out_recv.at[index], place.y * 2 + place.half, shard).start()

    @pl.loop(0, 8)
    def _(step):
        turn = step // 2
        z_step = turn + (turn // 2) * (5 - 2 * turn)
        z = (place.z + z_step) % 4

        @pl.when(step == 1)
        def _():
            for near in (1, 3):
                wait_bytes(dst, next_recv.at[near])
            relay(place.x, 0)
            for near in (1, 3):
                to_sibling(block(near, place.x), near)

        @pl.when(step == 2)
        def _():
            for near in (1, 3):
                wait_bytes(dst, next2_recv.at[near])
            relay(side_x, 1)
            for near in (1, 3):
                to_sibling(block(near, side_x), near)

        @pl.when(step == 6)
        def _():
            for far, x in ((0, place.x), (1, side_x)):
                wait_bytes(dst, far_recv.at[far])
                to_sibling(block(2, x), 2)

        @pl.when(step % 2 == 1)
        def _():
            wait_bytes(p_ref.at[pl.ds(0, tile), :], sib_recv.at[z_step])

        rows = rows_of(z * 2 + (place.core + step) % 2, tile)
        out_grad = dot_nt(p_ref[rows, :], w_ref[...])
        outs = []
        for head in range(2):
            cols = slice(head * HD, (head + 1) * HD)
            q = q_ref[rows, cols]
            scores = dot_nt(q, k_ref[:, cols])
            top = jnp.max(scores, axis=-1, keepdims=True)
            weights = jnp.exp2((scores - top) * EXP2_SCALE).astype(jnp.bfloat16)
            sums = dot_nn(weights, v_ones[head])
            inverse = 1.0 / sums[:, HD:]
            out = sums[:, :HD] * inverse
            grad = (out_grad[:, cols] * inverse).astype(jnp.bfloat16)
            delta = jnp.sum(grad.astype(jnp.float32) * out, axis=-1, keepdims=True)
            prob_grad = dot_nt(grad, v_ref[:, cols]) - delta
            score_grad = (weights.astype(jnp.float32) * prob_grad).astype(jnp.bfloat16)
            dq_out[rows, cols] = (dot_nn(score_grad, k_ref[:, cols]) * SCALE).astype(jnp.bfloat16)
            dk_sum[head] += dot_nn(q.T, score_grad)
            dv_sum[head] += dot_nn(grad.T, weights)
            outs.append(out.astype(jnp.bfloat16))
        turned[:, rows] = jnp.concatenate(outs, axis=1).T

        @pl.loop(0, 2)
        def _(index):
            send_rows(dq_out, gq_ref, z * 4 + ((place.core + step) % 2) * 2 + index, 0)

    for head in range(2):
        cols = slice(head * HD, (head + 1) * HD)
        dk_out[:, cols] = (dk_sum[head] * SCALE).astype(jnp.bfloat16).T

    @pl.loop(0, SHARDS)
    def _(step):
        send_rows(dk_out, gk_ref, (place.ctx + step) % SHARDS, 1)

    for head in range(2):
        cols = slice(head * HD, (head + 1) * HD)
        dv_out[:, cols] = dv_sum[head].astype(jnp.bfloat16).T

    @pl.loop(0, SHARDS)
    def _(step):
        send_rows(dv_out, gv_ref, (place.ctx + step) % SHARDS, 2)

    wide = width // 4

    @pl.loop(1, 5)
    def _(step):
        y = (place.y + step) % 4
        g_out[y] = dot_nn(turned[...], p_ref[:, rows_of(y, wide)]).astype(jnp.bfloat16)

        @pl.when(step < 4)
        def _():
            remote(
                g_out.at[y], g_in.at[place.y], g_send, g_recv, y * 2 + place.core, place.ctx
            ).start()

    g_in[place.y] = g_out[place.y]
    wait_bytes(g_in.at[pl.ds(0, 3)], g_recv)
    total = jnp.sum(g_in[...].astype(jnp.float32), axis=0)
    g_pair[0] = total[:, : wide // 2].astype(jnp.bfloat16)
    g_pair[1] = total[:, wide // 2 :].astype(jnp.bfloat16)

    @pl.when(place.away == 0)
    def _():
        remote(g_pair.at[1 - place.core], g_last.at[0], h_send.at[0], h_recv.at[0], sibling, place.ctx).start()
        g_last[0] = g_pair[place.core]

    @pl.when(place.away == 1)
    def _():
        for core in range(2):
            remote(
                g_pair.at[core], g_last.at[1], h_send.at[core], h_recv.at[1], place.y * 2 + core, place.mirror
            ).start()
        wait_bytes(g_last.at[0], h_recv.at[0])

    wait_bytes(g_last.at[1], h_recv.at[1])
    gp_ref[...] = g_last[0].astype(jnp.float32) + g_last[1].astype(jnp.float32)

    wait_bytes(g_pair.at[0], h_send.at[0])

    @pl.when(place.away == 1)
    def _():
        wait_bytes(g_pair.at[1], h_send.at[1])

    wait_bytes(g_out.at[pl.ds(0, 3)], g_send)
    for index, ref in enumerate((gq_ref, gk_ref, gv_ref)):
        wait_bytes(ref, out_recv.at[index])

        @pl.loop(0, SHARDS - 1 + place.away)
        def _(step):
            wait_bytes(dq_out.at[pl.ds(0, tokens), :], out_send.at[index])

    wait_bytes(p_ref.at[pl.ds(0, 4 * tokens), :], ag_send.at[0])
    wait_bytes(p_ref.at[pl.ds(0, 9 * tokens), :], ag_send.at[1])
    wait_bytes(p_ref.at[pl.ds(0, 2 * tokens), :], ag_send.at[2])


def run_attention(query, key, value, proj_rows, own, tokens, features):
    seq = query.shape[0]
    width = own.shape[1]
    vmem = pl.BlockSpec(memory_space=pltpu.VMEM)
    hbm = pl.BlockSpec(memory_space=pl.ANY)
    grad = jax.ShapeDtypeStruct((1, tokens, features), jnp.bfloat16)
    dma = pltpu.SemaphoreType.DMA
    low = jnp.bfloat16
    return pl.pallas_call(
        attention_kernel,
        out_shape=[grad, grad, grad, jax.ShapeDtypeStruct((PAIR, width // 8), jnp.float32)],
        in_specs=[vmem] * 4 + [hbm],
        out_specs=[hbm] * 3 + [vmem],
        scratch_shapes=[
            pltpu.VMEM((seq, width), low),
            pltpu.VMEM((2, seq, PAIR), low),
            pltpu.VMEM((2, HD, seq), jnp.float32),
            pltpu.VMEM((2, HD, seq), jnp.float32),
            pltpu.VMEM((PAIR, seq), low),
            pltpu.VMEM((seq, PAIR), low),
            pltpu.VMEM((seq, PAIR), low),
            pltpu.VMEM((seq, PAIR), low),
            pltpu.VMEM((4, PAIR, width // 4), low),
            pltpu.VMEM((4, PAIR, width // 4), low),
            pltpu.VMEM((2, PAIR, width // 8), low),
            pltpu.VMEM((2, PAIR, width // 8), low),
            dma((3,)), dma, dma((4,)), dma((4,)), dma((2,)), dma((4,)), dma,
            dma((3,)), dma((3,)), dma, dma, dma((2,)), dma((2,)),
        ],
        compiler_params=pltpu.CompilerParams(
            collective_id=1, has_side_effects=True, vmem_limit_bytes=63 * 2**20
        ),
    )(query, key, value, proj_rows, own)


def per_device(
    query, key_states, value_states, block_out, gate_mod, head_mod, head_weight, proj_weight, uncond_pred, target
):
    query_heads, key_heads, value_heads, proj_rows, own, grad_stream, loss = run_head(
        query, key_states, value_states, block_out, gate_mod, head_mod, head_weight, proj_weight, uncond_pred, target
    )
    grads = run_attention(
        query_heads, key_heads, value_heads, proj_rows, own, query.shape[1], query.shape[2]
    )
    return (grads[0], grads[1], grads[2], grad_stream, grads[3], loss[0, 0:1])


def solution(mesh):
    return jax.shard_map(
        per_device,
        mesh=mesh,
        in_specs=(
            P("dp", "ctx", None),
            P("dp", "ctx", None),
            P("dp", "ctx", None),
            P("dp", "ctx", None),
            P("dp", None),
            P("dp", None, None),
            P(),
            P("ctx", "dp"),
            P("dp", "ctx", None),
            P("dp", "ctx", None),
        ),
        out_specs=(
            P("dp", "ctx", None),
            P("dp", "ctx", None),
            P("dp", "ctx", None),
            P("dp", "ctx", None),
            P("ctx", "dp"),
            P("dp"),
        ),
        check_vma=False,
    )
```

time: 632 us -> 238 us (0.38); the launches traced: 622 us -> 238 us
  matrix products: 228 us -> 0 us
  Pallas kernels: 0 us -> 225 us
  other arithmetic: 119 us -> 0 us
  local copies, waits for them, and re-layouts: 105 us -> 12.2 us
  blocking collectives: 63.7 us -> 0 us
  waiting for transfers between devices: 43.2 us -> 0 us
  starting transfers between devices: 37.2 us -> 0 us
  between operations: 22.4 us -> 0.66 us
    pallas_call x0 -> x2, Pallas kernels: none -> 225 us  [the longest x1 155 us: run_attention(): pl.pallas_call(attention_kernel, out_shape=[grad, grad, grad, jax.ShapeDt...]
    dot_general x24 -> x0, matrix products: 199 us -> none  [the longest x4 74 us: step(): jnp.einsum('hqk,qhd->khd', score_grad, query_block, preferred_element_typ...]
    unnamed x8 -> x0, other arithmetic: 105 us -> none
    psum x2 -> x0, blocking collectives: 63.7 us -> none  [the longest x1 35.3 us: per_device(): lax.psum(jnp.stack([jnp.sum(cond_pred), jnp.sum(cond_pred * cond_pred), j...]
    unnamed x47 -> x15, local copies, waits for them, and re-layouts: 68.5 us -> 11 us
    all_to_all x6 -> x0, starting transfers between devices: 36.7 us -> none  [the longest x1 6.92 us: per_device(): lax.all_to_all(grad_keys[None], 'ctx', split_axis=1, concat_axis=2, tiled...]
    all_gather x2 -> x0, waiting for transfers between devices: 32.9 us -> none  [the longest x1 32.8 us: per_device(): lax.all_gather((gate_row * stream_grad_local).astype(jnp.bfloat16), 'ctx'...]
    sub x4 -> x0, matrix products: 29.3 us -> none  [step(): attn_probs = jax.nn.softmax(scores, axis=-1)]
  transfers between devices with their start and end apart: 9 -> 0, of which waited for: 2 -> 0; matrix products, arithmetic and copies ran while one was open for 34% -> 0% of each run, Pallas kernels for 0% -> 0%
where the time goes in v1:
time: 238 us
  Pallas kernels  225 us (95%)
  local copies, waits for them, and re-layouts  12.2 us (5%)
    pallas_call x1, Pallas kernels, run_attention(): pl.pallas_call(attention_kernel, out_shape=[grad, grad, grad, jax.ShapeDt...  155 us
    pallas_call x1, Pallas kernels, run_head(): pl.pallas_call(head_kernel, out_shape=[slab, slab, slab, jax.ShapeDtypeSt...  69.8 us
    unnamed x15, local copies, waits for them, and re-layouts  11 us

profile of v1, /device:TPU:1, one launch (start us, length us, event | category | flops | bytes accessed | tf_op | source)
XLA Modules:
  0.0 237.8 jit_solution(11530339732932907981)
XLA Ops:
  0.6 1.5 copy.16.uncond_ref
  2.1 1.5 copy.17.target_ref
  3.6 69.8 %shard_map.145 = (bf16[2048,256]{1,0:T(8,128)(2,1)}, bf16[2048,256]{1,0:T(8,128)(2,1)}, bf16[2048,256]{1,0:T(8,128)(2,1)}, bf16[256,5120]{1,0:T(8,128)(2,1)}, bf...) custom-call(bf16[1,128,4096]{2,1,0:T(8,128)(2,1)} %q_ref.1, bf16[1,128,4096]{2,1,0:T(8,128)(2,1)} %k_ref.1, ...), custom_call_target="tpu_custom_call" | custom-call | tf_op jit(solution)/shard_map/pallas_call | solution.py:237
  73.4 1.2 slice.3
  74.6 155.1 %shard_map.146 = (bf16[1,128,4096]{2,1,0:T(8,128)(2,1)}, bf16[1,128,4096]{2,1,0:T(8,128)(2,1)}, bf16[1,128,4096]{2,1,0:T(8,128)(2,1)}, f32[256,640]{1,0:T(8,128)}) custom-call(bf16[2048,256]{1,0:T(8,128)(2,1)} %get-tuple-element.17.q_ref, bf16[2048,256]{1,0:T(8,128)(2,1)} %get-tuple-element.18.k_ref, bf16[2048,256]{1,0:T(8,128)(2,1)} %get-tuple-element.19.v_ref, ...), custom_call_target="tpu_custom_call" | custom-call | tf_op jit(solution)/shard_map/pallas_call | solution.py:474
  229.7 0.0 copy-start.2
  229.8 2.4 copy.23
  232.1 0.0 copy-done.2
  232.1 0.0 copy-start.1
  232.1 1.0 copy.24
  233.1 0.6 copy-done.1
  233.7 0.0 copy-start
  233.7 1.0 copy.25
  234.7 0.7 copy-done
  235.4 0.0 copy-start.3
  235.4 1.1 copy.26
  236.5 0.5 copy-done.3
  237.0 0.8 copy.27
Async XLA Ops:
  229.7 2.4 %copy-start.2 = (bf16[1,128,4096]{2,1,0:T(8,128)(2,1)S(1)}, bf16[1,128,4096]{2,1,0:T(8,128)(2,1)}, u32[]{:S(2)}) copy-start(bf16[1,128,4096]{2,1,0:T(8,128)(2,1)} %get-tuple-element.35) | copy-start | bytes 3145732
  232.1 1.6 copy-start.1
  233.7 1.7 copy-start
  235.4 1.5 copy-start.3

commit v2 on v1

v2 whole, which is shorter than its diff:
```python
import functools

import jax
import jax.numpy as jnp
from jax import lax
from jax.experimental import pallas as pl
from jax.experimental.pallas import tpu as pltpu
from jax.sharding import PartitionSpec as P

HD = 128
PAIR = 2 * HD
SHARDS = 16
SCALE = 1.0 / float(HD) ** 0.5
EXP2_SCALE = 1.4426950408889634 * SCALE
MESH = pl.DeviceIdType.MESH

guidance = 5.0
rescale_mix = 0.7
norm_epsilon = 1e-06
spread_epsilon = 1e-05


def dot_nt(left, right):
    return lax.dot_general(left, right, (((1,), (1,)), ((), ())), preferred_element_type=jnp.float32)


def dot_nn(left, right):
    return lax.dot_general(left, right, (((1,), (0,)), ((), ())), preferred_element_type=jnp.float32)


def sigma_of(first_sum, square_sum, cell_count):
    mean_value = first_sum / cell_count
    return jnp.sqrt(square_sum / cell_count - mean_value * mean_value + spread_epsilon)


class Place:
    def __init__(self):
        dp = lax.axis_index("dp")
        ctx = lax.axis_index("ctx")
        self.dp, self.ctx = dp, ctx
        self.y, self.core = dp // 2, dp % 2
        self.z, self.x = ctx // 4, ctx % 4
        self.half = self.x // 2
        self.away = (self.core + self.half) % 2
        self.slot = self.z * 4 + self.x + self.away * (3 - 2 * self.x)
        self.mirror = self.z * 4 + 3 - self.x


def slot_of(z, x, core):
    away = (core + x // 2) % 2
    return z * 4 + x + away * (3 - 2 * x)


def greet(place):
    barrier = pltpu.get_barrier_semaphore()

    @pl.loop(0, 2 * SHARDS)
    def _(index):
        core, ctx = index // SHARDS, index % SHARDS
        own = jnp.logical_and(core == place.core, ctx == place.ctx)

        @pl.when(jnp.logical_not(own))
        def _():
            pl.semaphore_signal(
                barrier, inc=1, device_id=(place.y * 2 + core, ctx), device_id_type=MESH
            )

    for step in range(1, 4):
        other = ((place.y + step) % 4) * 2 + place.core
        pl.semaphore_signal(barrier, inc=1, device_id=(other, place.ctx), device_id_type=MESH)
    pl.semaphore_wait(barrier, 2 * SHARDS - 1 + 3)


def remote(src, dst, send_sem, recv_sem, dp, ctx):
    return pltpu.make_async_remote_copy(
        src_ref=src, dst_ref=dst, send_sem=send_sem, recv_sem=recv_sem, device_id=(dp, ctx), device_id_type=MESH
    )


def wait_bytes(ref, sem):
    pltpu.make_async_copy(ref, ref, sem).wait()


def rows_of(index, count):
    return pl.ds(pl.multiple_of(index * count, count), count)


def kernel(
    q_arg, k_arg, v_arg, stream_ref, gate_ref, mod_ref, hw_ref, pw_ref, uncond_ref, target_ref,
    gq_ref, gk_ref, gv_ref, gs_ref, gp_ref, loss_ref,
    q_ref, k_ref, v_ref, w_ref, p_ref, p_buf, moments, losses, mine, mine_loss,
    v_ones, kept, kept_out, kept_inverse, dk_sum, dv_sum, turned, g_out, g_in, g_pair, g_last,
    a2a_send, a2a_recv, w_send, w_recv, m_send, m_recv, l_send, l_recv, p_send, p_recv,
    ag_send, own_send, side_recv, own_x_recv, side_x_recv, far_x_recv, near_z_recv, far_z_recv, side_z_recv, sib_recv,
    out_send, out_recv, g_send, g_recv, h_send, h_recv,
):
    place = Place()
    tokens = stream_ref.shape[1]
    seq, width = p_ref.shape
    chunk = pw_ref.shape[1]
    cell_count = float(seq * uncond_ref.shape[1])
    half = tokens // 2
    tile = 2 * tokens
    first_cols = (width // 128 * 11 // 20) * 128
    x_cols, z_cols = pl.ds(0, first_cols), pl.ds(first_cols, width - first_cols)
    greet(place)

    def send_heads(src, dst, index):
        @pl.loop(0, SHARDS)
        def _(step):
            z = (place.z + step // 4) % 4
            x = 2 * place.core + (step // 2 + place.x) % 2
            core = (step + place.core) % 2
            slot = slot_of(z, x, core)
            own = jnp.logical_and(core == place.core, z * 4 + x == place.ctx)
            part = src.at[0, :, rows_of(slot, PAIR)]
            land = dst.at[rows_of(place.ctx, tokens), :]

            @pl.when(own)
            def _():
                pltpu.make_async_copy(part, land, a2a_recv.at[index]).start()

            @pl.when(jnp.logical_not(own))
            def _():
                remote(part, land, a2a_send.at[index], a2a_recv.at[index], place.y * 2 + core, z * 4 + x).start()

    own_cols = w_ref.at[:, rows_of(place.dp, chunk)]
    user = place.y * 2 + place.half

    @pl.when(place.away == 0)
    def _():
        pltpu.make_async_copy(pw_ref, own_cols, w_recv.at[0]).start()

    @pl.when(place.away == 1)
    def _():
        remote(pw_ref, own_cols, w_send.at[0], w_recv.at[0], user, place.ctx).start()

    remote(pw_ref, own_cols, w_send.at[1], w_recv.at[0], user, place.mirror).start()
    send_heads(q_arg, q_ref, 0)

    step_cols = PAIR
    pieces = [slice(start, start + step_cols) for start in range(0, width, step_cols)]

    def values(cols):
        return stream_ref[0, :, cols].astype(jnp.float32)

    def row_mean(term):
        folded = jnp.zeros((tokens, HD), jnp.float32)
        for cols in pieces:
            piece = term(cols)
            folded += piece[:, :HD] + piece[:, HD:]
        return jnp.sum(folded, axis=-1, keepdims=True) / width

    center = row_mean(values)
    inverse = lax.rsqrt(row_mean(lambda cols: jnp.square(values(cols) - center)) + norm_epsilon)

    def normed(cols):
        return (values(cols) - center) * inverse

    for cols in pieces:
        hidden = normed(cols) * (1.0 + mod_ref[0, 1:2, cols]) + mod_ref[0, 0:1, cols]
        p_buf[:, cols] = hidden.astype(jnp.bfloat16)
    cond_pred = dot_nt(p_buf[...], hw_ref[...]).T
    uncond = uncond_ref[0]
    target = target_ref[0]
    guided = uncond + guidance * (cond_pred - uncond)

    def total(array):
        return jnp.sum(jnp.sum(array, axis=0, keepdims=True), axis=1, keepdims=True)

    lane = lax.broadcasted_iota(jnp.int32, (8, 128), 1)
    tally = jnp.zeros((8, 128), jnp.float32)
    for index, array in enumerate(
        (cond_pred, cond_pred * cond_pred, guided, guided * guided, guided * target)
    ):
        tally = jnp.where(lane == index, total(array), tally)
    mine[...] = tally

    def share(src, dst, send, recv):
        @pl.loop(1, SHARDS)
        def _(step):
            ctx = (place.ctx + step) % SHARDS
            remote(src, dst.at[place.ctx], send, recv, place.dp, ctx).start()

    def settle(dst, send, recv):
        wait_bytes(dst.at[pl.ds(0, SHARDS - 1)], recv)
        wait_bytes(dst.at[pl.ds(0, SHARDS - 1)], send)

    moments[place.ctx] = tally
    share(mine, moments, m_send, m_recv)

    @pl.when(place.away == 0)
    def _():
        send_heads(k_arg, k_ref, 1)


    settle(moments, m_send, m_recv)
    sums = jnp.sum(moments[...], axis=0)
    sum_cond, square_cond, sum_guided, square_guided, cross = [sums[0:1, i : i + 1] for i in range(5)]
    sigma_cond = sigma_of(sum_cond, square_cond, cell_count)
    sigma_guided = sigma_of(sum_guided, square_guided, cell_count)
    mix_ratio = rescale_mix * sigma_cond / sigma_guided + (1.0 - rescale_mix)
    final = mix_ratio * guided
    final_grad = 2.0 * (final - target)
    loss_tile = jnp.broadcast_to(total(jnp.square(final - target)), (8, 128))
    mine_loss[...] = loss_tile
    losses[place.ctx] = loss_tile
    slope_sum = 2.0 * (mix_ratio * square_guided - cross)
    guided_coef = slope_sum * rescale_mix * sigma_cond / (cell_count * sigma_guided * sigma_guided * sigma_guided)
    guided_grad = mix_ratio * final_grad - guided_coef * (guided - sum_guided / cell_count)
    cond_coef = slope_sum * rescale_mix / (cell_count * sigma_guided * sigma_cond)
    cond_grad = (guidance * guided_grad + cond_coef * (cond_pred - sum_cond / cell_count)).astype(jnp.bfloat16)
    cond_rows = cond_grad.T

    def head_grad(cols):
        return dot_nn(cond_rows, hw_ref[:, cols]) * (1.0 + mod_ref[0, 1:2, cols])

    mean_one = row_mean(head_grad)
    mean_two = row_mean(lambda cols: head_grad(cols) * normed(cols))
    for cols in pieces:
        stream_grad = (head_grad(cols) - mean_one - normed(cols) * mean_two) * inverse
        p_buf[:, cols] = (gate_ref[:, cols] * stream_grad).astype(jnp.bfloat16)
        gs_ref[0, :, cols] = stream_grad.astype(jnp.bfloat16)

    side_x = place.x + 1 - 2 * (place.x % 2)
    side = place.z * 4 + side_x
    sibling = place.dp + 1 - 2 * place.core
    x_send, z_send = ag_send.at[0], ag_send.at[1]

    def beside(step):
        return ((place.z + step) % 4) * 4 + place.x

    def start(z_step, x):
        return slot_of((place.z + z_step) % 4, x, place.core) * tokens

    def part(z_step, x, cols, offset=0, count=None):
        return p_ref.at[pl.ds(pl.multiple_of(start(z_step, x) + offset, half), count or tokens), cols]

    def hand(ref, send, recv, dp, ctx):
        remote(ref, ref, send, recv, dp, ctx).start()

    def to_neighbours(ref, send, recv):
        hand(ref, send, recv.at[3], place.dp, beside(1))
        hand(ref, send, recv.at[1], place.dp, beside(3))

    def relay(x, cols, send, recv):
        hand(part(3, x, cols, 0, half), send, recv, place.dp, beside(1))
        hand(part(1, x, cols, half, half), send, recv, place.dp, beside(3))

    def to_sibling(ref, send, z_step):
        hand(ref, send, sib_recv.at[z_step], sibling, place.ctx)

    own = p_ref.at[pl.ds(pl.multiple_of(start(0, place.x), tokens), tokens), :]

    @pl.when(place.away == 0)
    def _():
        pltpu.make_async_copy(p_buf, own, p_recv).start()

    @pl.when(place.away == 1)
    def _():
        land = p_ref.at[rows_of(place.ctx, tokens), :]
        remote(p_buf, land, p_send, p_recv, sibling, place.mirror).start()

    @pl.when(place.away == 0)
    def _():
        send_heads(v_arg, v_ref, 2)


    pair = w_ref.at[:, rows_of(place.y, 2 * chunk)]
    wait_bytes(pair, w_recv.at[0])
    for step in range(1, 4):
        other = ((place.y + step) % 4) * 2 + place.core
        remote(pair, pair, w_send.at[2], w_recv.at[1], other, place.ctx).start()

    wait_bytes(own, p_recv)
    hand(part(0, place.x, x_cols), x_send, side_recv, place.dp, side)
    to_neighbours(part(0, place.x, z_cols), z_send, near_z_recv)
    to_neighbours(part(0, place.x, x_cols), x_send, own_x_recv)
    hand(part(0, place.x, z_cols), z_send, side_z_recv.at[0], place.dp, side)
    hand(own, own_send, sib_recv.at[0], sibling, place.ctx)
    share(mine_loss, losses, l_send, l_recv)

    @pl.when(place.away == 1)
    def _():
        wait_bytes(p_buf, p_send)
        send_heads(k_arg, k_ref, 1)
        send_heads(v_arg, v_ref, 2)


    def rows_at(z_step, which):
        return rows_of(((place.z + z_step) % 4) * 2 + which, tile)

    def forward(rows, keep):
        outs = []
        for head in range(2):
            cols = slice(head * HD, (head + 1) * HD)
            scores = dot_nt(q_ref[rows, cols], k_ref[:, cols])
            top = jnp.max(scores, axis=-1, keepdims=True)
            weights = jnp.exp2((scores - top) * EXP2_SCALE).astype(jnp.bfloat16)
            kept[keep, head] = weights
            sums = dot_nn(weights, v_ones[head])
            inverse = 1.0 / sums[:, HD:]
            out = sums[:, :HD] * inverse
            kept_out[keep, head] = out
            kept_inverse[keep, head] = inverse
            outs.append(out.astype(jnp.bfloat16))
        turned[:, rows] = jnp.concatenate(outs, axis=1).T

    def backward(rows, keep):
        out_grad = dot_nt(p_ref[rows, :], w_ref[...])
        for head in range(2):
            cols = slice(head * HD, (head + 1) * HD)
            q = q_ref[rows, cols]
            grad = (out_grad[:, cols] * kept_inverse[keep, head]).astype(jnp.bfloat16)
            delta = jnp.sum(grad.astype(jnp.float32) * kept_out[keep, head], axis=-1, keepdims=True)
            prob_grad = dot_nt(grad, v_ref[:, cols]) - delta
            weights = kept[keep, head]
            score_grad = (weights.astype(jnp.float32) * prob_grad).astype(jnp.bfloat16)
            dk_sum[head] += dot_nn(q.T, score_grad)
            dv_sum[head] += dot_nn(grad.T, weights)
            q_ref[rows, cols] = (dot_nn(score_grad, k_ref[:, cols]) * SCALE).astype(jnp.bfloat16)

    for near in (1, 3):
        wait_bytes(part(near, place.x, z_cols), near_z_recv.at[near])
    hand(part(1, place.x, z_cols), z_send, side_z_recv.at[1], place.dp, side)
    for near in (1, 3):
        to_sibling(part(near, place.x, z_cols), z_send, near)
    wait_bytes(part(0, side_x, x_cols), side_recv)
    to_neighbours(part(0, side_x, x_cols), x_send, side_x_recv)
    to_sibling(part(0, side_x, x_cols), x_send, 0)

    wait_bytes(part(0, side_x, z_cols), side_z_recv.at[0])
    hand(part(3, place.x, z_cols), z_send, side_z_recv.at[3], place.dp, side)
    relay(place.x, z_cols, z_send, far_z_recv)
    to_sibling(part(0, side_x, z_cols), z_send, 0)
    for near in (1, 3):
        wait_bytes(part(near, place.x, x_cols), own_x_recv.at[near])
    for near in (1, 3):
        to_sibling(part(near, place.x, x_cols), x_send, near)

    dk_sum[...] = jnp.zeros_like(dk_sum)
    dv_sum[...] = jnp.zeros_like(dv_sum)
    for index, ref in enumerate((q_ref, k_ref, v_ref)):
        wait_bytes(ref, a2a_recv.at[index])
    for head in range(2):
        v_ones[head, :, 0:HD] = v_ref[:, head * HD : (head + 1) * HD]
        v_ones[head, :, HD : 2 * HD] = jnp.ones((seq, HD), jnp.bfloat16)

    @pl.loop(0, 2)
    def _(which):
        forward(rows_at(2, which), which)

    wait_bytes(w_ref.at[:, pl.ds(0, 6 * chunk)], w_recv.at[1])

    @pl.loop(0, 6)
    def _(step):
        turn = step // 2
        z_step = turn + turn // 2

        @pl.when(step == 2)
        def _():
            wait_bytes(part(2, place.x, z_cols), far_z_recv)
            relay(place.x, x_cols, x_send, far_x_recv.at[0])
            hand(part(2, place.x, z_cols), z_send, side_z_recv.at[2], place.dp, side)
            to_sibling(part(2, place.x, z_cols), z_send, 2)
            wait_bytes(part(1, side_x, z_cols), side_z_recv.at[1])
            to_sibling(part(1, side_x, z_cols), z_send, 1)
            for near in (1, 3):
                wait_bytes(part(near, side_x, x_cols), side_x_recv.at[near])
            relay(side_x, x_cols, x_send, far_x_recv.at[1])
            for near in (1, 3):
                to_sibling(part(near, side_x, x_cols), x_send, near)

        @pl.when(step == 4)
        def _():
            wait_bytes(part(3, side_x, z_cols), side_z_recv.at[3])
            to_sibling(part(3, side_x, z_cols), z_send, 3)

        @pl.when(step % 2 == 1)
        def _():
            wait_bytes(p_ref.at[pl.ds(0, tile), :], sib_recv.at[z_step])

        rows = rows_at(z_step, (place.core + step) % 2)
        forward(rows, 2)
        backward(rows, 2)

    for far, x in ((0, place.x), (1, side_x)):
        wait_bytes(part(2, x, x_cols), far_x_recv.at[far])
        to_sibling(part(2, x, x_cols), x_send, 2)
    wait_bytes(part(2, side_x, z_cols), side_z_recv.at[2])
    to_sibling(part(2, side_x, z_cols), z_send, 2)

    def send_rows(src, dst_ref, shard, index):
        own_shard = jnp.logical_and(place.away == 0, shard == place.ctx)
        rows = src.at[rows_of(shard, tokens), :]
        land = dst_ref.at[0, :, rows_of(place.slot, PAIR)]

        @pl.when(own_shard)
        def _():
            pltpu.make_async_copy(rows, land, out_recv.at[index]).start()

        @pl.when(jnp.logical_not(own_shard))
        def _():
            remote(rows, land, out_send.at[index], out_recv.at[index], user, shard).start()

    @pl.loop(0, 12)
    def _(step):
        turn = step // 4
        send_rows(q_ref, gq_ref, ((place.z + turn + turn // 2) % 4) * 4 + (step + place.x) % 4, 0)

    wait_bytes(p_ref.at[pl.ds(0, tile), :], sib_recv.at[2])

    wide = width // 4

    @pl.loop(1, 5)
    def _(step):
        y = (place.y + step) % 4
        g_out[y] = dot_nn(turned[...], p_ref[:, rows_of(y, wide)]).astype(jnp.bfloat16)

        @pl.when(step < 4)
        def _():
            remote(g_out.at[y], g_in.at[place.y], g_send, g_recv, y * 2 + place.core, place.ctx).start()

    g_in[place.y] = g_out[place.y]

    @pl.loop(0, 2)
    def _(which):
        backward(rows_at(2, which), which)

    @pl.loop(0, 4)
    def _(step):
        send_rows(q_ref, gq_ref, ((place.z + 2) % 4) * 4 + (step + place.x) % 4, 0)

    for head in range(2):
        cols = slice(head * HD, (head + 1) * HD)
        k_ref[:, cols] = (dk_sum[head] * SCALE).astype(jnp.bfloat16).T

    @pl.loop(0, SHARDS)
    def _(step):
        send_rows(k_ref, gk_ref, (place.ctx + step) % SHARDS, 1)

    for head in range(2):
        cols = slice(head * HD, (head + 1) * HD)
        v_ref[:, cols] = dv_sum[head].astype(jnp.bfloat16).T

    @pl.loop(0, SHARDS)
    def _(step):
        send_rows(v_ref, gv_ref, (place.ctx + step) % SHARDS, 2)

    settle(losses, l_send, l_recv)
    loss_ref[...] = jnp.sum(losses[...], axis=0) / cell_count

    wait_bytes(g_in.at[pl.ds(0, 3)], g_recv)
    total_g = jnp.sum(g_in[...].astype(jnp.float32), axis=0)
    g_pair[0] = total_g[:, : wide // 2].astype(jnp.bfloat16)
    g_pair[1] = total_g[:, wide // 2 :].astype(jnp.bfloat16)

    @pl.when(place.away == 0)
    def _():
        remote(g_pair.at[1 - place.core], g_last.at[0], h_send.at[0], h_recv.at[0], sibling, place.ctx).start()
        g_last[0] = g_pair[place.core]

    @pl.when(place.away == 1)
    def _():
        for core in range(2):
            remote(
                g_pair.at[core], g_last.at[1], h_send.at[core], h_recv.at[1], place.y * 2 + core, place.mirror
            ).start()
        wait_bytes(g_last.at[0], h_recv.at[0])

    wait_bytes(g_last.at[1], h_recv.at[1])
    gp_ref[...] = g_last[0].astype(jnp.float32) + g_last[1].astype(jnp.float32)

    for index, ref in enumerate((gq_ref, gk_ref, gv_ref)):
        wait_bytes(ref, out_recv.at[index])

    @pl.loop(0, SHARDS - 1 + place.away)
    def _(step):
        for index in range(3):
            wait_bytes(q_ref.at[pl.ds(0, tokens), :], a2a_send.at[index])
            wait_bytes(q_ref.at[pl.ds(0, tokens), :], out_send.at[index])

    wait_bytes(g_pair.at[0], h_send.at[0])
    wait_bytes(g_out.at[pl.ds(0, 3)], g_send)
    wait_bytes(w_ref.at[:, pl.ds(0, chunk)], w_send.at[1])
    wait_bytes(w_ref.at[:, pl.ds(0, 6 * chunk)], w_send.at[2])

    @pl.when(place.away == 1)
    def _():
        wait_bytes(g_pair.at[1], h_send.at[1])
        wait_bytes(w_ref.at[:, pl.ds(0, chunk)], w_send.at[0])

    wait_bytes(p_buf, own_send)
    wait_bytes(p_ref.at[pl.ds(0, 14 * tokens), x_cols], x_send)
    wait_bytes(p_ref.at[pl.ds(0, 14 * tokens), z_cols], z_send)


def hand_over(*refs):
    sources, loss, results, loss_out = refs[:5], refs[5], refs[6:11], refs[11]
    held, arrived, left = refs[12:17], refs[17], refs[18]
    fetches = [pltpu.make_async_copy(sources[i], held[i], arrived.at[i]) for i in range(5)]
    stores = [pltpu.make_async_copy(held[i], results[i], left.at[i]) for i in range(5)]
    for fetch in fetches:
        fetch.start()
    loss_out[0] = loss[0, 0]
    for fetch, store in zip(fetches, stores):
        fetch.wait()
        store.start()
    for store in stores:
        store.wait()


def per_device(
    query, key_states, value_states, block_out, gate_mod, head_mod, head_weight, proj_weight, uncond_pred, target
):
    tokens, features = query.shape[1:]
    seq = tokens * SHARDS
    width = block_out.shape[2]
    vmem = pl.BlockSpec(memory_space=pltpu.VMEM)
    hbm = pl.BlockSpec(memory_space=pl.ANY)
    grad = jax.ShapeDtypeStruct(query.shape, jnp.bfloat16)
    dma = pltpu.SemaphoreType.DMA
    low, wide = jnp.bfloat16, jnp.float32
    grads = pl.pallas_call(
        kernel,
        out_shape=[
            grad, grad, grad,
            jax.ShapeDtypeStruct(block_out.shape, low),
            jax.ShapeDtypeStruct(proj_weight.shape, wide),
            jax.ShapeDtypeStruct((8, 128), wide),
        ],
        in_specs=[hbm] * 3 + [vmem] * 7,
        out_specs=[hbm] * 3 + [vmem] * 3,
        scratch_shapes=[
            pltpu.VMEM((seq, PAIR), low),
            pltpu.VMEM((seq, PAIR), low),
            pltpu.VMEM((seq, PAIR), low),
            pltpu.VMEM((PAIR, width), low),
            pltpu.VMEM((seq, width), low),
            pltpu.VMEM((tokens, width), low),
            pltpu.VMEM((SHARDS, 8, 128), wide),
            pltpu.VMEM((SHARDS, 8, 128), wide),
            pltpu.VMEM((8, 128), wide),
            pltpu.VMEM((8, 128), wide),
            pltpu.VMEM((2, seq, PAIR), low),
            pltpu.VMEM((3, 2, 2 * tokens, seq), low),
            pltpu.VMEM((3, 2, 2 * tokens, HD), wide),
            pltpu.VMEM((3, 2, 2 * tokens, HD), wide),
            pltpu.VMEM((2, HD, seq), wide),
            pltpu.VMEM((2, HD, seq), wide),
            pltpu.VMEM((PAIR, seq), low),
            pltpu.VMEM((4, PAIR, width // 4), low),
            pltpu.VMEM((4, PAIR, width // 4), low),
            pltpu.VMEM((2, PAIR, width // 8), low),
            pltpu.VMEM((2, PAIR, width // 8), low),
            dma((3,)), dma((3,)), dma((3,)), dma((2,)),
            dma, dma, dma, dma, dma, dma,
            dma((2,)), dma, dma, dma((4,)), dma((4,)), dma((2,)), dma((4,)), dma, dma((4,)), dma((4,)),
            dma((3,)), dma((3,)), dma, dma, dma((2,)), dma((2,)),
        ],
        compiler_params=pltpu.CompilerParams(
            collective_id=0, has_side_effects=True, vmem_limit_bytes=63 * 2**20
        ),
    )(
        query, key_states, value_states, block_out, gate_mod, head_mod, head_weight, proj_weight,
        jnp.swapaxes(uncond_pred, 1, 2), jnp.swapaxes(target, 1, 2),
    )
    smem = pl.BlockSpec(memory_space=pltpu.SMEM)
    return pl.pallas_call(
        hand_over,
        out_shape=[jax.ShapeDtypeStruct(array.shape, array.dtype) for array in grads[:5]]
        + [jax.ShapeDtypeStruct((1,), wide)],
        in_specs=[hbm] * 5 + [smem],
        out_specs=[hbm] * 5 + [smem],
        scratch_shapes=[pltpu.VMEM(array.shape, array.dtype) for array in grads[:5]] + [dma((5,)), dma((5,))],
        compiler_params=pltpu.CompilerParams(vmem_limit_bytes=63 * 2**20),
    )(*grads)


def solution(mesh):
    return jax.shard_map(
        per_device,
        mesh=mesh,
        in_specs=(
            P("dp", "ctx", None),
            P("dp", "ctx", None),
            P("dp", "ctx", None),
            P("dp", "ctx", None),
            P("dp", None),
            P("dp", None, None),
            P(),
            P("ctx", "dp"),
            P("dp", "ctx", None),
            P("dp", "ctx", None),
        ),
        out_specs=(
            P("dp", "ctx", None),
            P("dp", "ctx", None),
            P("dp", "ctx", None),
            P("dp", "ctx", None),
            P("ctx", "dp"),
            P("dp"),
        ),
        check_vma=False,
    )
```

time: 238 us -> 194 us (0.82)
  Pallas kernels: 225 us -> 193 us
  local copies, waits for them, and re-layouts: 12.2 us -> 0 us
    pallas_call x2, Pallas kernels: 225 us -> 193 us  [the longest x1 188 us: per_device(): pl.pallas_call(kernel, out_shape=[grad, grad, grad, jax.ShapeDtypeStruct(...]
    unnamed x15 -> x0, local copies, waits for them, and re-layouts: 11 us -> none
where the time goes in v2:
time: 194 us
  Pallas kernels  193 us (99%)
    pallas_call x1, Pallas kernels, per_device(): pl.pallas_call(kernel, out_shape=[grad, grad, grad, jax.ShapeDtypeStruct(...  188 us
    pallas_call x1, Pallas kernels, per_device(): pl.pallas_call(hand_over, out_shape=[jax.ShapeDtypeStruct(array.shape, ar...  5.32 us

profile of v2, /device:TPU:1, one launch (start us, length us, event | category | flops | bytes accessed | tf_op | source)
XLA Modules:
  0.0 194.1 jit_solution(3142603867064710993)
XLA Ops:
  0.6 188.0 %shard_map.145 = (bf16[1,128,4096]{2,1,0:T(8,128)(2,1)}, bf16[1,128,4096]{2,1,0:T(8,128)(2,1)}, bf16[1,128,4096]{2,1,0:T(8,128)(2,1)}, bf16[1,128,5120]{2,1,0:T(...) custom-call(bf16[1,128,4096]{2,1,0:T(8,128)(2,1)} %q_arg.1, bf16[1,128,4096]{2,1,0:T(8,128)(2,1)} %k_arg.1, ...), custom_call_target="tpu_custom_call" | custom-call | tf_op jit(solution)/shard_map/pallas_call | solution.py:524
  188.6 5.3 %shard_map.146 = (bf16[1,128,4096]{2,1,0:T(8,128)(2,1)}, bf16[1,128,4096]{2,1,0:T(8,128)(2,1)}, bf16[1,128,4096]{2,1,0:T(8,128)(2,1)}, bf16[1,128,5120]{2,1,0:T(...) custom-call(bf16[1,128,4096]{2,1,0:T(8,128)(2,1)} %get-tuple-element.12.refs_0_, ...), custom_call_target="tpu_custom_call" | custom-call | tf_op jit(solution)/shard_map/pallas_call | solution.py:569

commit v3 on v2

--- a/solution.py
+++ b/solution.py
@@ -89,7 +89,7 @@
     q_arg, k_arg, v_arg, stream_ref, gate_ref, mod_ref, hw_ref, pw_ref, uncond_ref, target_ref,
     gq_ref, gk_ref, gv_ref, gs_ref, gp_ref, loss_ref,
     q_ref, k_ref, v_ref, w_ref, p_ref, p_buf, moments, losses, mine, mine_loss,
-    v_ones, kept, kept_out, kept_inverse, dk_sum, dv_sum, turned, g_out, g_in, g_pair, g_last,
+    v_ones, last_grad, kept, kept_out, kept_inverse, dk_sum, dv_sum, turned, g_out, g_in, g_pair, g_last,
     a2a_send, a2a_recv, w_send, w_recv, m_send, m_recv, l_send, l_recv, p_send, p_recv,
     ag_send, own_send, side_recv, own_x_recv, side_x_recv, far_x_recv, near_z_recv, far_z_recv, side_z_recv, sib_recv,
     out_send, out_recv, g_send, g_recv, h_send, h_recv,
@@ -101,7 +101,7 @@
     cell_count = float(seq * uncond_ref.shape[1])
     half = tokens // 2
     tile = 2 * tokens
-    first_cols = (width // 128 * 11 // 20) * 128
+    first_cols = (width // 128 * 28 // 40) * 128
     x_cols, z_cols = pl.ds(0, first_cols), pl.ds(first_cols, width - first_cols)
     greet(place)
 
@@ -306,19 +306,22 @@
             outs.append(out.astype(jnp.bfloat16))
         turned[:, rows] = jnp.concatenate(outs, axis=1).T
 
+    def backward_head(rows, keep, head, out_grad):
+        cols = slice(head * HD, (head + 1) * HD)
+        q = q_ref[rows, cols]
+        grad = (out_grad * kept_inverse[keep, head]).astype(jnp.bfloat16)
+        delta = jnp.sum(grad.astype(jnp.float32) * kept_out[keep, head], axis=-1, keepdims=True)
+        prob_grad = dot_nt(grad, v_ref[:, cols]) - delta
+        weights = kept[keep, head]
+        score_grad = (weights.astype(jnp.float32) * prob_grad).astype(jnp.bfloat16)
+        dk_sum[head] += dot_nn(q.T, score_grad)
+        dv_sum[head] += dot_nn(grad.T, weights)
+        q_ref[rows, cols] = (dot_nn(score_grad, k_ref[:, cols]) * SCALE).astype(jnp.bfloat16)
+
     def backward(rows, keep):
         out_grad = dot_nt(p_ref[rows, :], w_ref[...])
         for head in range(2):
-            cols = slice(head * HD, (head + 1) * HD)
-            q = q_ref[rows, cols]
-            grad = (out_grad[:, cols] * kept_inverse[keep, head]).astype(jnp.bfloat16)
-            delta = jnp.sum(grad.astype(jnp.float32) * kept_out[keep, head], axis=-1, keepdims=True)
-            prob_grad = dot_nt(grad, v_ref[:, cols]) - delta
-            weights = kept[keep, head]
-            score_grad = (weights.astype(jnp.float32) * prob_grad).astype(jnp.bfloat16)
-            dk_sum[head] += dot_nn(q.T, score_grad)
-            dv_sum[head] += dot_nn(grad.T, weights)
-            q_ref[rows, cols] = (dot_nn(score_grad, k_ref[:, cols]) * SCALE).astype(jnp.bfloat16)
+            backward_head(rows, keep, head, out_grad[:, head * HD : (head + 1) * HD])
 
     for near in (1, 3):
         wait_bytes(part(near, place.x, z_cols), near_z_recv.at[near])
@@ -390,10 +393,10 @@
     wait_bytes(part(2, side_x, z_cols), side_z_recv.at[2])
     to_sibling(part(2, side_x, z_cols), z_send, 2)
 
-    def send_rows(src, dst_ref, shard, index):
+    def send_rows(src, dst_ref, shard, index, start=0, count=PAIR):
         own_shard = jnp.logical_and(place.away == 0, shard == place.ctx)
-        rows = src.at[rows_of(shard, tokens), :]
-        land = dst_ref.at[0, :, rows_of(place.slot, PAIR)]
+        rows = src.at[rows_of(shard, tokens), pl.ds(start, count)]
+        land = dst_ref.at[0, :, pl.ds(pl.multiple_of(place.slot * PAIR + start, HD), count)]
 
         @pl.when(own_shard)
         def _():
@@ -412,41 +415,40 @@
 
     wide = width // 4
 
-    @pl.loop(1, 5)
+    def proj_part(y):
+        return dot_nn(turned[...], p_ref[:, rows_of(y, wide)]).astype(jnp.bfloat16)
+
+    @pl.loop(0, 3)
     def _(step):
-        y = (place.y + step) % 4
-        g_out[y] = dot_nn(turned[...], p_ref[:, rows_of(y, wide)]).astype(jnp.bfloat16)
-
-        @pl.when(step < 4)
-        def _():
-            remote(g_out.at[y], g_in.at[place.y], g_send, g_recv, y * 2 + place.core, place.ctx).start()
-
-    g_in[place.y] = g_out[place.y]
+        y = (place.y + 2 + step + step // 2) % 4
+        g_out[y] = proj_part(y)
+        remote(g_out.at[y], g_in.at[place.y], g_send, g_recv, y * 2 + place.core, place.ctx).start()
 
     @pl.loop(0, 2)
     def _(which):
-        backward(rows_at(2, which), which)
+        last_grad[which] = dot_nt(p_ref[rows_at(2, which), :], w_ref[...])
+
+    for head in range(2):
+        cols = slice(head * HD, (head + 1) * HD)
+
+        @pl.loop(0, 2)
+        def _(which):
+            backward_head(rows_at(2, which), which, head, last_grad[which, :, cols])
+
+        k_ref[:, cols] = (dk_sum[head] * SCALE).astype(jnp.bfloat16).T
+        v_ref[:, cols] = dv_sum[head].astype(jnp.bfloat16).T
+
+        @pl.loop(0, SHARDS)
+        def _(step):
+            shard = (place.ctx + step) % SHARDS
+            send_rows(k_ref, gk_ref, shard, 1, head * HD, HD)
+            send_rows(v_ref, gv_ref, shard, 2, head * HD, HD)
 
     @pl.loop(0, 4)
     def _(step):
         send_rows(q_ref, gq_ref, ((place.z + 2) % 4) * 4 + (step + place.x) % 4, 0)
 
-    for head in range(2):
-        cols = slice(head * HD, (head + 1) * HD)
-        k_ref[:, cols] = (dk_sum[head] * SCALE).astype(jnp.bfloat16).T
-
-    @pl.loop(0, SHARDS)
-    def _(step):
-        send_rows(k_ref, gk_ref, (place.ctx + step) % SHARDS, 1)
-
-    for head in range(2):
-        cols = slice(head * HD, (head + 1) * HD)
-        v_ref[:, cols] = dv_sum[head].astype(jnp.bfloat16).T
-
-    @pl.loop(0, SHARDS)
-    def _(step):
-        send_rows(v_ref, gv_ref, (place.ctx + step) % SHARDS, 2)
-
+    g_in[place.y] = proj_part(place.y)
     settle(losses, l_send, l_recv)
     loss_ref[...] = jnp.sum(losses[...], axis=0) / cell_count
 
@@ -543,6 +545,7 @@
             pltpu.VMEM((8, 128), wide),
             pltpu.VMEM((8, 128), wide),
             pltpu.VMEM((2, seq, PAIR), low),
+            pltpu.VMEM((2, 2 * tokens, PAIR), wide),
             pltpu.VMEM((3, 2, 2 * tokens, seq), low),
             pltpu.VMEM((3, 2, 2 * tokens, HD), wide),
             pltpu.VMEM((3, 2, 2 * tokens, HD), wide),

time: 194 us -> 184 us (0.948)
  Pallas kernels: 193 us -> 183 us
    pallas_call x1, Pallas kernels: 188 us -> 178 us  [per_device(): pl.pallas_call(kernel, out_shape=[grad, grad, grad, jax.ShapeDtypeStruct(...]
where the time goes in v3:
time: 184 us
  Pallas kernels  183 us (99%)
    pallas_call x1, Pallas kernels, per_device(): pl.pallas_call(kernel, out_shape=[grad, grad, grad, jax.ShapeDtypeStruct(...  178 us
    pallas_call x1, Pallas kernels, per_device(): pl.pallas_call(hand_over, out_shape=[jax.ShapeDtypeStruct(array.shape, ar...  5.32 us

profile of v3, /device:TPU:1, one launch (start us, length us, event | category | flops | bytes accessed | tf_op | source)
XLA Modules:
  0.0 184.0 jit_solution(16641530591851470291)
XLA Ops:
  0.6 177.9 %shard_map.145 = (bf16[1,128,4096]{2,1,0:T(8,128)(2,1)}, bf16[1,128,4096]{2,1,0:T(8,128)(2,1)}, bf16[1,128,4096]{2,1,0:T(8,128)(2,1)}, bf16[1,128,5120]{2,1,0:T(...) custom-call(bf16[1,128,4096]{2,1,0:T(8,128)(2,1)} %q_arg.1, bf16[1,128,4096]{2,1,0:T(8,128)(2,1)} %k_arg.1, ...), custom_call_target="tpu_custom_call" | custom-call | tf_op jit(solution)/shard_map/pallas_call | solution.py:526
  178.5 5.3 %shard_map.146 = (bf16[1,128,4096]{2,1,0:T(8,128)(2,1)}, bf16[1,128,4096]{2,1,0:T(8,128)(2,1)}, bf16[1,128,4096]{2,1,0:T(8,128)(2,1)}, bf16[1,128,5120]{2,1,0:T(...) custom-call(bf16[1,128,4096]{2,1,0:T(8,128)(2,1)} %get-tuple-element.12.refs_0_, ...), custom_call_target="tpu_custom_call" | custom-call | tf_op jit(solution)/shard_map/pallas_call | solution.py:572

commit v4 on v3

--- a/solution.py
+++ b/solution.py
@@ -135,8 +135,11 @@
     def _():
         remote(pw_ref, own_cols, w_send.at[0], w_recv.at[0], user, place.ctx).start()
 
-    remote(pw_ref, own_cols, w_send.at[1], w_recv.at[0], user, place.mirror).start()
-    send_heads(q_arg, q_ref, 0)
+
+    @pl.when(place.away == 0)
+    def _():
+        send_heads(q_arg, q_ref, 0)
+
 
     step_cols = PAIR
     pieces = [slice(start, start + step_cols) for start in range(0, width, step_cols)]
@@ -266,12 +269,6 @@
         send_heads(v_arg, v_ref, 2)
 
 
-    pair = w_ref.at[:, rows_of(place.y, 2 * chunk)]
-    wait_bytes(pair, w_recv.at[0])
-    for step in range(1, 4):
-        other = ((place.y + step) % 4) * 2 + place.core
-        remote(pair, pair, w_send.at[2], w_recv.at[1], other, place.ctx).start()
-
     wait_bytes(own, p_recv)
     hand(part(0, place.x, x_cols), x_send, side_recv, place.dp, side)
     to_neighbours(part(0, place.x, z_cols), z_send, near_z_recv)
@@ -283,9 +280,18 @@
     @pl.when(place.away == 1)
     def _():
         wait_bytes(p_buf, p_send)
+        send_heads(q_arg, q_ref, 0)
         send_heads(k_arg, k_ref, 1)
         send_heads(v_arg, v_ref, 2)
 
+
+    remote(pw_ref, own_cols, w_send.at[1], w_recv.at[0], user, place.mirror).start()
+
+    pair = w_ref.at[:, rows_of(place.y, 2 * chunk)]
+    wait_bytes(pair, w_recv.at[0])
+    for step in range(1, 4):
+        other = ((place.y + step) % 4) * 2 + place.core
+        remote(pair, pair, w_send.at[2], w_recv.at[1], other, place.ctx).start()
 
     def rows_at(z_step, which):
         return rows_of(((place.z + z_step) % 4) * 2 + which, tile)

time: 184 us -> 176 us (0.957)
  Pallas kernels: 183 us -> 175 us
    pallas_call x1, Pallas kernels: 178 us -> 170 us  [per_device(): pl.pallas_call(kernel, out_shape=[grad, grad, grad, jax.ShapeDtypeStruct(...]
where the time goes in v4:
time: 176 us
  Pallas kernels  175 us (99%)
    pallas_call x1, Pallas kernels, per_device(): pl.pallas_call(kernel, out_shape=[grad, grad, grad, jax.ShapeDtypeStruct(...  170 us
    pallas_call x1, Pallas kernels, per_device(): pl.pallas_call(hand_over, out_shape=[jax.ShapeDtypeStruct(array.shape, ar...  5.32 us

profile of v4, /device:TPU:1, one launch (start us, length us, event | category | flops | bytes accessed | tf_op | source)
XLA Modules:
  0.0 176.3 jit_solution(12527932358449929574)
XLA Ops:
  0.6 170.2 %shard_map.145 = (bf16[1,128,4096]{2,1,0:T(8,128)(2,1)}, bf16[1,128,4096]{2,1,0:T(8,128)(2,1)}, bf16[1,128,4096]{2,1,0:T(8,128)(2,1)}, bf16[1,128,5120]{2,1,0:T(...) custom-call(bf16[1,128,4096]{2,1,0:T(8,128)(2,1)} %q_arg.1, bf16[1,128,4096]{2,1,0:T(8,128)(2,1)} %k_arg.1, ...), custom_call_target="tpu_custom_call" | custom-call | tf_op jit(solution)/shard_map/pallas_call | solution.py:532
  170.8 5.3 %shard_map.146 = (bf16[1,128,4096]{2,1,0:T(8,128)(2,1)}, bf16[1,128,4096]{2,1,0:T(8,128)(2,1)}, bf16[1,128,4096]{2,1,0:T(8,128)(2,1)}, bf16[1,128,5120]{2,1,0:T(...) custom-call(bf16[1,128,4096]{2,1,0:T(8,128)(2,1)} %get-tuple-element.12.refs_0_, ...), custom_call_target="tpu_custom_call" | custom-call | tf_op jit(solution)/shard_map/pallas_call | solution.py:578
